TPU v7x, 32 devices: a whole 2x2x4 slice. The times are simulated.
32 devices in a mesh: dp: 32 (over z, y, x, core).
Axes of the slice: x: 2, y: 2, z: 4, core: 2. Of those that a mesh axis runs over, the one named last changes fastest.
Arguments:
- tokens: bfloat16 [512, 14, 14, 512], P('dp'), may hold values from -6 to 6
- cotangent: bfloat16 [512, 14, 14, 512], P('dp'), may hold values from -6 to 6
- counts: int32 [32], P('dp'), may hold values from 8 to 16, as said below
- region_ids: int32 [14, 14], replicated, may hold values from 0 to 2
- relative_index: int32 [49, 49], replicated, may hold values from 0 to 168
- attn_gain: bfloat16 [512], P('dp'), may hold values from 0.5 to 1.5
- attn_shift: bfloat16 [512], P('dp'), may hold values from -3 to 3
- qkv_weight: bfloat16 [512, 1536], P('dp'), may hold values from -0.25 to 0.25
- query_bias: bfloat16 [512], P('dp'), may hold values from -3 to 3
- value_bias: bfloat16 [512], P('dp'), may hold values from -3 to 3
- proj_weight: bfloat16 [512, 512], P('dp'), may hold values from -0.75 to 0.75
- proj_bias: bfloat16 [512], P('dp'), may hold values from -3 to 3
- mlp_gain: bfloat16 [512], P('dp'), may hold values from 0.5 to 1.5
- mlp_shift: bfloat16 [512], P('dp'), may hold values from -3 to 3
- hidden_weight: bfloat16 [512, 2048], P('dp'), may hold values from -0.25 to 0.25
- hidden_bias: bfloat16 [2048], P('dp'), may hold values from -3 to 3
- output_weight: bfloat16 [2048, 512], P('dp'), may hold values from -0.125 to 0.125
- output_bias: bfloat16 [512], P('dp'), may hold values from -3 to 3
- bias_table: bfloat16 [169, 16], replicated, may hold values from -4 to 4
Outputs:
- activations: bfloat16 [512, 14, 14, 512], P('dp')
- tokens_grad: bfloat16 [512, 14, 14, 512], P('dp')
- attn_gain_grad: float32 [512], P('dp')
- attn_shift_grad: float32 [512], P('dp')
- qkv_weight_grad: float32 [512, 1536], P('dp')
- query_bias_grad: float32 [512], P('dp')
- value_bias_grad: float32 [512], P('dp')
- proj_weight_grad: float32 [512, 512], P('dp')
- proj_bias_grad: float32 [512], P('dp')
- mlp_gain_grad: float32 [512], P('dp')
- mlp_shift_grad: float32 [512], P('dp')
- hidden_weight_grad: float32 [512, 2048], P('dp')
- hidden_bias_grad: float32 [2048], P('dp')
- output_weight_grad: float32 [2048, 512], P('dp')
- output_bias_grad: float32 [512], P('dp')
- bias_table_grad: float32 [169, 16], replicated
Inputs may be any that keep to these rules, and one draw needn't show every extreme that they name: `counts`: each device holds between 8 and 16 images in its first slots; in every draw some device holds 16 and some holds 8.
All inputs are finite; a program needn't handle non-finite values.
Results may differ from a plain program's by a relative error of at most 0.011.
Values may be sent and summed in bfloat16 or wider, within the bound.
A program may use at most 320 MiB of HBM per device.

v0:
```python
import math

import jax
import jax.numpy as jnp
from jax import lax
from jax.sharding import PartitionSpec as P

WIN = 7
MAP = 14
SHIFT = 3


EPS = 1e-05
MASK_FILL = -100.0


def normalize(rows):
    mean = jnp.mean(rows, axis=-1, keepdims=True)
    centred = rows - mean
    inverse = lax.rsqrt(jnp.mean(centred * centred, axis=-1, keepdims=True) + EPS)
    return (centred * inverse, inverse)


def norm_back(grad_normed, normed, inverse):
    first_mean = jnp.mean(grad_normed, axis=-1, keepdims=True)
    second_mean = jnp.mean(grad_normed * normed, axis=-1, keepdims=True)
    return inverse * (grad_normed - first_mean - normed * second_mean)


def to_windows(field):
    images = field.shape[0]
    count = MAP // WIN
    rolled = jnp.roll(field, (-SHIFT, -SHIFT), axis=(1, 2))
    blocks = rolled.reshape(images, count, WIN, count, WIN, field.shape[-1])
    return blocks.transpose(0, 1, 3, 2, 4, 5).reshape(
        images, count * count, WIN * WIN, field.shape[-1]
    )


def from_windows(blocks):
    images = blocks.shape[0]
    count = MAP // WIN
    grid = blocks.reshape(images, count, count, WIN, WIN, blocks.shape[-1])
    grid = grid.transpose(0, 1, 3, 2, 4, 5).reshape(images, MAP, MAP, blocks.shape[-1])
    return jnp.roll(grid, (SHIFT, SHIFT), axis=(1, 2))


def region_mask(region_ids):
    count = MAP // WIN
    cells = (
        region_ids.reshape(count, WIN, count, WIN)
        .transpose(0, 2, 1, 3)
        .reshape(count * count, WIN * WIN)
    )
    same = cells[:, :, None] == cells[:, None, :]
    return jnp.where(same, 0.0, MASK_FILL).astype(jnp.float32)


def attention_scores(queries, keys, position, mask):
    raw = jnp.einsum("bwqhe,bwkhe->bwhqk", queries, keys, preferred_element_type=jnp.float32)
    return raw * queries.shape[-1] ** (-0.5) + position[None, None] + mask[None, :, None]


def gelu_slope(hidden):
    cumulative = 0.5 * (1.0 + lax.erf(hidden * (1.0 / math.sqrt(2.0))))
    density = jnp.exp(-0.5 * hidden * hidden) * (1.0 / math.sqrt(2.0 * math.pi))
    return cumulative + hidden * density


def row_total(values):
    return jnp.sum(values, axis=0, dtype=jnp.float32)


def transposed_dot(left, right):
    return lax.dot_general(
        left, right, (((0,), (0,)), ((), ())), preferred_element_type=jnp.float32
    )


def local(
    tokens,
    cotangent,
    counts,
    region_ids,
    relative_index,
    attn_gain,
    attn_shift,
    qkv_weight,
    query_bias,
    value_bias,
    proj_weight,
    proj_bias,
    mlp_gain,
    mlp_shift,
    hidden_weight,
    hidden_bias,
    output_weight,
    output_bias,
    bias_table,
):
    gathered = (
        lax.all_gather(attn_gain, "dp", axis=0, tiled=True),
        lax.all_gather(attn_shift, "dp", axis=0, tiled=True),
        lax.all_gather(qkv_weight, "dp", axis=0, tiled=True),
        lax.all_gather(query_bias, "dp", axis=0, tiled=True),
        lax.all_gather(value_bias, "dp", axis=0, tiled=True),
        lax.all_gather(proj_weight, "dp", axis=0, tiled=True),
        lax.all_gather(proj_bias, "dp", axis=0, tiled=True),
        lax.all_gather(mlp_gain, "dp", axis=0, tiled=True),
        lax.all_gather(mlp_shift, "dp", axis=0, tiled=True),
        lax.all_gather(hidden_weight, "dp", axis=0, tiled=True),
        lax.all_gather(hidden_bias, "dp", axis=0, tiled=True),
        lax.all_gather(output_weight, "dp", axis=0, tiled=True),
        lax.all_gather(output_bias, "dp", axis=0, tiled=True),
    )
    (
        gain_one,
        shift_one,
        qkv_full,
        query_add,
        value_add,
        proj_full,
        proj_add,
        gain_two,
        shift_two,
        hidden_full,
        hidden_add,
        out_full,
        out_add,
    ) = gathered
    images = tokens.shape[0]
    width = tokens.shape[-1]
    heads = bias_table.shape[1]
    head_size = width // heads
    table_rows = bias_table.shape[0]
    span = WIN * WIN
    scale = head_size ** (-0.5)
    ordered = to_windows(tokens)
    window_count = ordered.shape[1]
    inputs = ordered.astype(jnp.float32).reshape(-1, width)
    valid = (jnp.arange(images) < counts[0]).astype(jnp.float32)
    row_valid = jnp.repeat(valid, MAP * MAP)[:, None]
    mask = region_mask(region_ids)
    one_hot = (relative_index.reshape(-1)[:, None] == jnp.arange(table_rows)[None, :]).astype(
        jnp.float32
    )
    position = (
        jnp.dot(
            one_hot,
            bias_table.astype(jnp.float32),
            precision=lax.Precision.HIGHEST,
            preferred_element_type=jnp.float32,
        )
        .reshape(span, span, heads)
        .transpose(2, 0, 1)
    )
    normed_one, inverse_one = normalize(inputs)
    first_in = (normed_one * gain_one.astype(jnp.float32) + shift_one.astype(jnp.float32)).astype(
        jnp.bfloat16
    )
    joined = jnp.concatenate([query_add, jnp.zeros_like(query_add), value_add]).astype(jnp.float32)
    qkv_rows = (jnp.dot(first_in, qkv_full, preferred_element_type=jnp.float32) + joined).astype(
        jnp.bfloat16
    )
    windows = qkv_rows.reshape(images, window_count, span, 3, heads, head_size)
    queries, keys, values = (windows[:, :, :, 0], windows[:, :, :, 1], windows[:, :, :, 2])
    scores = attention_scores(queries, keys, position, mask)
    log_total = jax.nn.logsumexp(scores, axis=-1, keepdims=True)
    probs_low = jnp.exp(scores - log_total).astype(jnp.bfloat16)
    mixed = jnp.einsum(
        "bwhqk,bwkhe->bwqhe", probs_low, values, preferred_element_type=jnp.float32
    ).astype(jnp.bfloat16)
    attended = mixed.reshape(-1, width)
    after_attn = (
        inputs
        + jnp.dot(attended, proj_full, preferred_element_type=jnp.float32)
        + proj_add.astype(jnp.float32)
    )
    normed_two, inverse_two = normalize(after_attn)
    second_in = (normed_two * gain_two.astype(jnp.float32) + shift_two.astype(jnp.float32)).astype(
        jnp.bfloat16
    )
    hidden = jnp.dot(
        second_in, hidden_full, preferred_element_type=jnp.float32
    ) + hidden_add.astype(jnp.float32)
    active = jax.nn.gelu(hidden, approximate=False).astype(jnp.bfloat16)
    outcome = (
        after_attn
        + jnp.dot(active, out_full, preferred_element_type=jnp.float32)
        + out_add.astype(jnp.float32)
    )
    activations = from_windows(
        (outcome * row_valid).astype(jnp.bfloat16).reshape(images, window_count, span, width)
    )
    regathered = (
        lax.all_gather(attn_gain, "dp", axis=0, tiled=True),
        lax.all_gather(attn_shift, "dp", axis=0, tiled=True),
        lax.all_gather(qkv_weight, "dp", axis=0, tiled=True),
        lax.all_gather(query_bias, "dp", axis=0, tiled=True),
        lax.all_gather(value_bias, "dp", axis=0, tiled=True),
        lax.all_gather(proj_weight, "dp", axis=0, tiled=True),
        lax.all_gather(proj_bias, "dp", axis=0, tiled=True),
        lax.all_gather(mlp_gain, "dp", axis=0, tiled=True),
        lax.all_gather(mlp_shift, "dp", axis=0, tiled=True),
        lax.all_gather(hidden_weight, "dp", axis=0, tiled=True),
        lax.all_gather(hidden_bias, "dp", axis=0, tiled=True),
        lax.all_gather(output_weight, "dp", axis=0, tiled=True),
        lax.all_gather(output_bias, "dp", axis=0, tiled=True),
    )
    (
        gain_one,
        shift_one,
        qkv_full,
        query_add,
        value_add,
        proj_full,
        proj_add,
        gain_two,
        shift_two,
        hidden_full,
        hidden_add,
        out_full,
        out_add,
    ) = regathered
    grad_out = to_windows(cotangent).astype(jnp.float32).reshape(-1, width) * row_valid
    grad_out_low = grad_out.astype(jnp.bfloat16)
    grad_out_weight = transposed_dot(active, grad_out_low)
    grad_out_bias = row_total(grad_out)
    grad_active = jnp.dot(grad_out_low, out_full.T, preferred_element_type=jnp.float32)
    grad_hidden = (grad_active * gelu_slope(hidden)).astype(jnp.bfloat16)
    grad_hidden_weight = transposed_dot(second_in, grad_hidden)
    grad_hidden_bias = row_total(grad_hidden)
    grad_second = jnp.dot(grad_hidden, hidden_full.T, preferred_element_type=jnp.float32)
    grad_gain_two = row_total(grad_second * normed_two)
    grad_shift_two = row_total(grad_second)
    grad_after = grad_out + norm_back(
        grad_second * gain_two.astype(jnp.float32), normed_two, inverse_two
    )
    grad_proj = grad_after.astype(jnp.bfloat16)
    grad_proj_weight = transposed_dot(attended, grad_proj)
    grad_proj_bias = row_total(grad_proj)
    grad_attended = jnp.dot(grad_proj, proj_full.T, preferred_element_type=jnp.float32).astype(
        jnp.bfloat16
    )
    grad_mixed = grad_attended.reshape(images, window_count, span, heads, head_size)
    again_scores = attention_scores(queries, keys, position, mask)
    probs = jnp.exp(again_scores - log_total)
    probs_again = probs.astype(jnp.bfloat16)
    grad_probs = jnp.einsum(
        "bwqhe,bwkhe->bwhqk", grad_mixed, values, preferred_element_type=jnp.float32
    )
    grad_values = jnp.einsum(
        "bwhqk,bwqhe->bwkhe", probs_again, grad_mixed, preferred_element_type=jnp.float32
    )
    inner = jnp.sum(grad_probs * probs, axis=-1, keepdims=True)
    grad_scores = (probs * (grad_probs - inner)).astype(jnp.bfloat16)
    grad_queries = (
        jnp.einsum("bwhqk,bwkhe->bwqhe", grad_scores, keys, preferred_element_type=jnp.float32)
        * scale
    )
    grad_keys = (
        jnp.einsum("bwhqk,bwqhe->bwkhe", grad_scores, queries, preferred_element_type=jnp.float32)
        * scale
    )
    grad_position = jnp.sum(grad_scores, axis=(0, 1), dtype=jnp.float32)
    grad_table = jnp.dot(
        one_hot.T,
        grad_position.transpose(1, 2, 0).reshape(span * span, heads),
        precision=lax.Precision.HIGHEST,
        preferred_element_type=jnp.float32,
    )
    grad_qkv = jnp.concatenate(
        [
            grad_queries.reshape(-1, width).astype(jnp.bfloat16),
            grad_keys.reshape(-1, width).astype(jnp.bfloat16),
            grad_values.reshape(-1, width).astype(jnp.bfloat16),
        ],
        axis=1,
    )
    grad_qkv_weight = transposed_dot(first_in, grad_qkv)
    grad_columns = row_total(grad_qkv)
    grad_query_bias = grad_columns[:width]
    grad_value_bias = grad_columns[2 * width :]
    grad_first = jnp.dot(grad_qkv, qkv_full.T, preferred_element_type=jnp.float32)
    grad_gain_one = row_total(grad_first * normed_one)
    grad_shift_one = row_total(grad_first)
    grad_inputs = grad_after + norm_back(
        grad_first * gain_one.astype(jnp.float32), normed_one, inverse_one
    )
    tokens_grad = from_windows(
        grad_inputs.astype(jnp.bfloat16).reshape(images, window_count, span, width)
    )
    owned = (
        lax.psum_scatter(grad_gain_one, "dp", scatter_dimension=0, tiled=True),
        lax.psum_scatter(grad_shift_one, "dp", scatter_dimension=0, tiled=True),
        lax.psum_scatter(grad_qkv_weight, "dp", scatter_dimension=0, tiled=True),
        lax.psum_scatter(grad_query_bias, "dp", scatter_dimension=0, tiled=True),
        lax.psum_scatter(grad_value_bias, "dp", scatter_dimension=0, tiled=True),
        lax.psum_scatter(grad_proj_weight, "dp", scatter_dimension=0, tiled=True),
        lax.psum_scatter(grad_proj_bias, "dp", scatter_dimension=0, tiled=True),
        lax.psum_scatter(grad_gain_two, "dp", scatter_dimension=0, tiled=True),
        lax.psum_scatter(grad_shift_two, "dp", scatter_dimension=0, tiled=True),
        lax.psum_scatter(grad_hidden_weight, "dp", scatter_dimension=0, tiled=True),
        lax.psum_scatter(grad_hidden_bias, "dp", scatter_dimension=0, tiled=True),
        lax.psum_scatter(grad_out_weight, "dp", scatter_dimension=0, tiled=True),
        lax.psum_scatter(grad_out_bias, "dp", scatter_dimension=0, tiled=True),
    )
    table_total = lax.psum(grad_table, "dp")
    return (
        activations,
        tokens_grad,
        owned[0],
        owned[1],
        owned[2],
        owned[3],
        owned[4],
        owned[5],
        owned[6],
        owned[7],
        owned[8],
        owned[9],
        owned[10],
        owned[11],
        owned[12],
        table_total,
    )


def solution(mesh):
    placed = (
        P("dp", None, None, None),
        P("dp", None, None, None),
        P("dp"),
        P(),
        P(),
        P("dp"),
        P("dp"),
        P("dp", None),
        P("dp"),
        P("dp"),
        P("dp", None),
        P("dp"),
        P("dp"),
        P("dp"),
        P("dp", None),
        P("dp"),
        P("dp", None),
        P("dp"),
        P(),
    )
    return jax.shard_map(
        local,
        mesh=mesh,
        in_specs=placed,
        out_specs=(
            P("dp", None, None, None),
            P("dp", None, None, None),
            P("dp"),
            P("dp"),
            P("dp", None),
            P("dp"),
            P("dp"),
            P("dp", None),
            P("dp"),
            P("dp"),
            P("dp"),
            P("dp", None),
            P("dp"),
            P("dp", None),
            P("dp"),
            P(),
        ),
        check_vma=False,
    )
```

profile of v0, /device:TPU:0, one launch (start us, length us, event | category | flops | bytes accessed | tf_op | source)
XLA Modules:
  0.0 1151.8 jit_solution(15547141884158413054)
XLA Ops:
  10.6 2.0 slice.71
  12.6 2.0 slice.83
  17.8 3.9 fusion.49
  21.8 6.0 multiply_reduce_fusion.1
  28.0 4.8 copy.130
  40.7 42.6 %all-reduce.19 = (bf16[512]{0:T(512)(128)(2,1)}, bf16[512]{0:T(512)(128)(2,1)}, bf16[512]{0:T(512)(128)(2,1)S(1)}, bf16[512]{0:T(512)(128)(2,1)S(1)}, bf16[512]{...) all-reduce(bf16[512]{0:T(512)(128)(2,1)S(1)} %dynamic-update-slice., ...), channel_id=1, replica_groups=mesh['dp'=32] {'dp'}, use_global_device_ids=true, to_apply=%add.3 | all-reduce | flops 6144 | bytes 24576
  90.1 2.0 copy.94
  92.1 45.6 %all_gather.50 = bf16[512,512]{1,0:T(8,128)(2,1)} all-gather(bf16[16,512]{1,0:T(8,128)(2,1)S(1)} %copy-done.31), channel_id=1, replica_groups=mesh['dp'=32] {'dp'}, dimensions={0}, use_global_device_ids=true | all-gather | bytes 540672 | tf_op jit(solution)/shard_map/all_gather | solution.py:107
  137.8 1.9 fusion.43
  141.7 4.9 copy.129
  146.6 7.8 reshape.206
  154.7 7.8 reshape.205
  162.7 10.8 add_convert_fusion
  173.5 41.9 %reshape.229 = bf16[16,4,49,3,16,32]{5,4,3,2,1,0:T(8,128)(2,1)} reshape(bf16[3136,1536]{1,0:T(8,128)(2,1)} %add_convert_fusion) | data formatting | bytes 19267584 | tf_op jit(solution)/shard_map/reshape | solution.py:165
  215.4 25.9 %fusion.57 = (bf16[16,4,49,1,16,32]{5,4,3,2,1,0:T(8,128)(2,1)}, bf16[16,4,49,1,16,32]{5,4,3,2,1,0:T(8,128)(2,1)}, bf16[16,4,49,1,16,32]{5,4,3,2,1,0:T(8,128)(2,1)}) fusion(bf16[16,4,49,3,16,32]{5,4,3,2,1,0:T(8,128)(2,1)} %reshape.229), kind=kLoop, calls=%fused_computation.122 | loop fusion | bytes 19267584 | tf_op jit(solution)/shard_map/slice | solution.py:166
  241.3 17.6 %copy.120 = bf16[16,4,49,1,16,32]{2,5,4,1,0,3:T(8,128)(2,1)} copy(bf16[16,4,49,1,16,32]{5,4,3,2,1,0:T(8,128)(2,1)} %get-tuple-element.47) | data formatting | bytes 6422528
  258.9 17.6 %copy.119 = bf16[16,4,49,1,16,32]{2,5,4,1,0,3:T(8,128)(2,1)} copy(bf16[16,4,49,1,16,32]{5,4,3,2,1,0:T(8,128)(2,1)} %get-tuple-element.48) | data formatting | bytes 6422528
  276.5 17.7 %copy.121 = bf16[16,4,49,1,16,32]{2,5,4,1,0,3:T(8,128)(2,1)} copy(bf16[16,4,49,1,16,32]{5,4,3,2,1,0:T(8,128)(2,1)} %get-tuple-element.49) | data formatting | bytes 6422528
  294.2 18.7 %fusion.59 = (f32[16,4,16,49]{3,2,1,0:T(8,128)S(1)}, f32[16,4,16,49,49]{3,4,2,1,0:T(8,128)}) fusion(f32[4,49,49]{1,2,0:T(8,128)S(1)} %compare_select_fusion, f32[16,49,49]{1,2,0:T(8,128)S(1)} %copy-done.17, bf16[16,4,49,1,16,32]{2,5,4,1,0,3:T(8,128)(2,1)} %copy.121, bf16[16,4,49,1,16,32]{2,5,4,1,0,3:T(8,128)(2,1)} %copy.120), kind=kOutput, calls=%fused_computation.124 | convolution fusion | flops 167136256 | bytes 16649808 | tf_op jit(solution)/shard_map/bwqhe,bwkhe->bwhqk/dot_general | solution.py:60
  312.9 15.9 %exponential_reduce_fusion = f32[16,4,16,49]{3,2,1,0:T(8,128)S(1)} fusion(f32[16,4,16,49,49]{3,4,2,1,0:T(8,128)} %get-tuple-element.53, f32[16,4,16,49]{3,2,1,0:T(8,128)S(1)} %is-finite_select_fusion), kind=kLoop, calls=%fused_computation.6 | loop fusion | flops 4867072 | bytes 10235904 | tf_op jit(solution)/shard_map/reduce_sum | solution.py:168
  329.0 16.7 %convert_bitcast_fusion.1 = bf16[16,4,49,16,32]{2,4,3,1,0:T(8,128)(2,1)} fusion(bf16[16,4,49,1,16,32]{2,5,4,1,0,3:T(8,128)(2,1)} %copy.119, f32[16,4,16,49,49]{3,4,2,1,0:T(8,128)} %get-tuple-element.53, f32[16,4,16,49]{3,2,1,0:T(8,128)S(1)} %log_add_fusion), kind=kOutput, calls=%fused_computation.47 | convolution fusion | flops 163874816 | bytes 16457728 | tf_op jit(solution)/shard_map/bwhqk,bwkhe->bwqhe/dot_general | solution.py:170
  345.7 12.1 %copy.97 = bf16[16,4,49,16,32]{2,1,0,4,3:T(4,128)(2,1)} copy(bf16[16,4,49,16,32]{2,4,3,1,0:T(8,128)(2,1)} %convert_bitcast_fusion.1) | data formatting | bytes 6422528 | tf_op jit(solution)/shard_map/convert_element_type | solution.py:172
  357.8 12.2 %reshape.200 = bf16[3136,512]{0,1:T(8,128)(2,1)S(1)} reshape(bf16[16,4,49,16,32]{2,1,0,4,3:T(4,128)(2,1)} %copy.97) | data formatting | bytes 6422528 | tf_op jit(solution)/shard_map/reshape | solution.py:173
  370.1 6.2 fusion.60
  376.3 2.7 copy-done.3
  380.4 64.0 %fusion.2 = (bf16[3136,2048]{1,0:T(8,128)(2,1)}, f32[3136,2048]{1,0:T(8,128)}) fusion(f32[2048]{0:T(1024)S(1)} %copy-done.39, bf16[512,2048]{1,0:T(8,128)(2,1)} %all-gather.6.cloned.1.call-done, f32[3136,512]{1,0:T(8,128)} %copy-done.3, f32[512]{0:T(512)S(1)} %copy-done.45, f32[512]{0:T(512)S(1)} %copy-done.36, f32[3136]{0:T(1024)S(1)} %add_rsqrt_fusion.1, ...), kind=kOutput, calls=%fused_computation.10 | convolution fusion | flops 7008583680 | bytes 47092224 | tf_op jit(solution)/shard_map/dot_general | solution.py:183
  444.4 23.1 %convert_reduce_fusion.1 = (f32[2048]{0:T(1024)}, bf16[3136,2048]{1,0:T(8,128)(2,1)}) fusion(f32[3136,2048]{1,0:T(8,128)} %get-tuple-element.57, f32[2048]{0:T(1024)S(1)} %copy-done.39, bf16[2048,512]{1,0:T(8,128)(2,1)} %all-gather.8.cloned.1.call-done, f32[3136,512]{1,0:T(8,128)} %reshape.206, f32[3136]{0:T(1024)S(1)} %copy-done.23), kind=kOutput, calls=%fused_computation.17 | convolution fusion | flops 6663370752 | bytes 47083776 | tf_op jit(solution)/shard_map/dot_general | solution.py:229
  467.5 15.7 %multiply_reduce_fusion.3 = (f32[512]{0:T(512)}, f32[3136]{0:T(1024)S(1)}, f32[3136]{0:T(1024)S(1)}, f32[512]{0:T(512)}, f32[3136,512]{1,0:T(8,128)}) fusion(f32[3136,512]{1,0:T(8,128)S(1)} %copy-done.4, f32[3136]{0:T(1024)S(1)} %add_rsqrt_fusion.1, f32[3136]{0:T(1024)S(1)} %broadcast_multiply_fusion.5, f32[512]{0:T(512)S(1)} %copy-done.36, ...), kind=kOutput, calls=%fused_computation.56 | convolution fusion | flops 6591112192 | bytes 27843584 | tf_op jit(solution)/shard_map/dot_general | solution.py:233
  483.2 7.3 convert_reduce_fusion.3
  490.6 2.7 copy-done.2
  493.3 2.9 fusion.50
  496.1 4.8 convolution_convert_fusion
  500.9 11.0 reshape.230
  511.9 17.7 %copy.101 = bf16[16,4,49,16,32]{2,4,3,1,0:T(8,128)(2,1)} copy(bf16[16,4,49,16,32]{4,3,2,1,0:T(8,128)(2,1)} %reshape.230) | data formatting | bytes 6422528 | tf_op jit(solution)/shard_map/reshape | solution.py:245
  529.5 17.9 %convert_bitcast_fusion = bf16[16,4,49,16,32]{2,4,3,1,0:T(8,128)(2,1)} fusion(bf16[16,4,49,16,32]{2,4,3,1,0:T(8,128)(2,1)} %copy.101, f32[16,4,16,49,49]{3,4,2,1,0:T(8,128)} %get-tuple-element.53, f32[16,4,16,49]{3,2,1,0:T(8,128)S(1)} %copy-done.12), kind=kOutput, calls=%fused_computation.46 | convolution fusion | flops 163874816 | bytes 16457728 | tf_op jit(solution)/shard_map/bwhqk,bwqhe->bwkhe/dot_general | solution.py:252
  547.5 25.1 %multiply_reduce_fusion = (f32[16,4,16,49]{3,2,1,0:T(8,128)S(1)}, f32[16,4,16,49,49]{3,4,2,1,0:T(8,128)}) fusion(f32[16,4,16,49,49]{3,4,2,1,0:T(8,128)} %get-tuple-element.53, f32[16,4,16,49]{3,2,1,0:T(8,128)S(1)} %copy-done.12, bf16[16,4,49,16,32]{2,4,3,1,0:T(8,128)(2,1)} %copy.101, bf16[16,4,49,1,16,32]{2,5,4,1,0,3:T(8,128)(2,1)} %copy.119), kind=kOutput, calls=%fused_computation.4 | convolution fusion | flops 164677632 | bytes 26492928 | tf_op jit(solution)/shard_map/bwqhe,bwkhe->bwhqk/dot_general | solution.py:249
  572.5 27.3 %convert_reduce_fusion = (f32[16,49,49]{1,2,0:T(8,128)}, bf16[16,4,16,49,49]{3,4,2,1,0:T(8,128)(2,1)}) fusion(f32[16,4,16,49,49]{3,4,2,1,0:T(8,128)} %get-tuple-element.60, f32[16,4,16,49]{3,2,1,0:T(8,128)S(1)} %get-tuple-element.59, f32[16,4,16,49,49]{3,4,2,1,0:T(8,128)} %get-tuple-element.53, f32[16,4,16,49]{3,2,1,0:T(8,128)S(1)} %copy-done.12), kind=kLoop, calls=%fused_computation.2 | loop fusion | flops 14713328 | bytes 25141312 | tf_op jit(solution)/shard_map/reduce_sum | solution.py:265
  599.9 14.2 %fusion.34 = bf16[16,4,49,16,32]{2,4,3,1,0:T(8,128)(2,1)} fusion(bf16[16,4,16,49,49]{3,4,2,1,0:T(8,128)(2,1)} %get-tuple-element.44, bf16[16,4,49,1,16,32]{2,5,4,1,0,3:T(8,128)(2,1)} %copy.120), kind=kOutput, calls=%fused_computation.75 | convolution fusion | flops 160563200 | bytes 11339776 | tf_op jit(solution)/shard_map/bwhqk,bwqhe->bwkhe/dot_general | solution.py:262
  614.0 12.2 %fusion.31 = bf16[16,4,49,16,32]{2,4,3,1,0:T(8,128)(2,1)} fusion(bf16[16,4,16,49,49]{3,4,2,1,0:T(8,128)(2,1)} %get-tuple-element.44, bf16[16,4,49,1,16,32]{2,5,4,1,0,3:T(8,128)(2,1)} %copy.121), kind=kOutput, calls=%fused_computation.74 | convolution fusion | flops 160563200 | bytes 11339776 | tf_op jit(solution)/shard_map/bwhqk,bwkhe->bwqhe/dot_general | solution.py:258
  626.3 12.2 %copy.103 = bf16[16,4,49,16,32]{2,1,0,4,3:T(4,128)(2,1)} copy(bf16[16,4,49,16,32]{2,4,3,1,0:T(8,128)(2,1)} %fusion.31) | data formatting | bytes 6422528 | tf_op jit(solution)/shard_map/convert_element_type | solution.py:274
  638.4 12.0 %convert_element_type.187 = bf16[3136,512]{0,1:T(8,128)(2,1)S(1)} reshape(bf16[16,4,49,16,32]{2,1,0,4,3:T(4,128)(2,1)} %copy.103) | data formatting | bytes 6422528 | tf_op jit(solution)/shard_map/convert_element_type | solution.py:274
  650.5 12.1 %copy.105 = bf16[16,4,49,16,32]{2,1,0,4,3:T(4,128)(2,1)} copy(bf16[16,4,49,16,32]{2,4,3,1,0:T(8,128)(2,1)} %fusion.34) | data formatting | bytes 6422528 | tf_op jit(solution)/shard_map/convert_element_type | solution.py:275
  662.6 13.3 %convert_element_type.190 = bf16[3136,512]{0,1:T(8,128)(2,1)} reshape(bf16[16,4,49,16,32]{2,1,0,4,3:T(4,128)(2,1)} %copy.105) | data formatting | bytes 6422528 | tf_op jit(solution)/shard_map/convert_element_type | solution.py:275
  676.0 1.9 constant_dynamic-update-slice_fusion.2
  679.1 2.0 constant_dynamic-update-slice_fusion.1
  681.1 12.1 %copy.108 = bf16[16,4,49,16,32]{2,1,0,4,3:T(4,128)(2,1)} copy(bf16[16,4,49,16,32]{2,4,3,1,0:T(8,128)(2,1)} %convert_bitcast_fusion) | data formatting | bytes 6422528 | tf_op jit(solution)/shard_map/convert_element_type | solution.py:276
  693.2 12.3 %convert_element_type.193 = bf16[3136,512]{0,1:T(8,128)(2,1)S(1)} reshape(bf16[16,4,49,16,32]{2,1,0,4,3:T(4,128)(2,1)} %copy.108) | data formatting | bytes 6422528 | tf_op jit(solution)/shard_map/convert_element_type | solution.py:276
  705.5 1.9 constant_dynamic-update-slice_fusion
  707.4 13.8 %fusion.54 = f32[512,1536]{1,0:T(8,128)} fusion(bf16[3136,1536]{0,1:T(8,128)(2,1)} %constant_dynamic-update-slice_fusion, f32[3136,512]{1,0:T(8,128)} %reshape.205, f32[512]{0:T(512)S(1)} %copy-done.48, f32[512]{0:T(512)S(1)} %copy-done.35, f32[3136]{0:T(1024)S(1)} %copy-done.29, f32[3136]{0:T(1024)S(1)} %copy-done.27), kind=kOutput, calls=%fused_computation.119 | convolution fusion | flops 4940529664 | bytes 19231232 | tf_op jit(solution)/shard_map/dot_general | solution.py:75
  721.4 13.6 %fusion.53 = f32[2048,512]{1,0:T(8,128)} fusion(bf16[3136,2048]{1,0:T(8,128)(2,1)} %get-tuple-element.56, f32[3136,512]{1,0:T(8,128)} %reshape.206, f32[3136]{0:T(1024)S(1)} %copy-done.23), kind=kOutput, calls=%fused_computation.118 | convolution fusion | flops 6579879936 | bytes 23474432 | tf_op jit(solution)/shard_map/dot_general | solution.py:75
  735.5 16.3 %fusion.55 = f32[512,2048]{1,0:T(8,128)} fusion(bf16[3136,2048]{1,0:T(8,128)(2,1)} %get-tuple-element.63, f32[3136,512]{1,0:T(8,128)} %copy-done.3, f32[512]{0:T(512)S(1)} %copy-done.46, f32[512]{0:T(512)S(1)} %copy-done.37, f32[3136]{0:T(1024)S(1)} %copy-done.25, f32[3136]{0:T(1024)S(1)} %copy-done.22), kind=kOutput, calls=%fused_computation.120 | convolution fusion | flops 6584696832 | bytes 23491072 | tf_op jit(solution)/shard_map/dot_general | solution.py:75
  752.9 12.1 %fusion.30 = bf16[3136,512]{1,0:T(8,128)(2,1)S(1)} fusion(f32[3136,512]{1,0:T(8,128)} %copy-done.3, bf16[3136,2048]{1,0:T(8,128)(2,1)} %get-tuple-element.56, bf16[2048,512]{1,0:T(8,128)(2,1)} %all-gather.8.cloned.1.call-done, f32[3136]{0:T(1024)S(1)} %copy-done.23, f32[512]{0:T(512)S(1)} %convert_element_type.173), kind=kOutput, calls=%fused_computation.71 | convolution fusion | flops 6583091200 | bytes 24590592 | tf_op jit(solution)/shard_map/dot_general | solution.py:189
  765.0 2.7 reshape_reshape.6
  767.7 4.3 copy.98
  774.6 14.6 %multiply_reduce_fusion.4 = (f32[512]{0:T(512)S(1)}, f32[3136]{0:T(1024)S(1)}, f32[3136]{0:T(1024)S(1)}, f32[512]{0:T(512)S(1)}, f32[3136,512]{1,0:T(8,128)}) fusion(f32[3136,512]{1,0:T(8,128)S(1)} %bitcast.98, f32[3136]{0:T(1024)S(1)} %copy-done.29, f32[3136]{0:T(1024)S(1)} %copy-done.27, f32[512]{0:T(512)S(1)} %copy-done.35, ...), kind=kOutput, calls=%fused_computation.58 | convolution fusion | flops 4946945024 | bytes 24108032 | tf_op jit(solution)/shard_map/dot_general | solution.py:284
  789.3 5.0 add_convert_fusion.1
  794.3 2.9 reshape_reshape.7
  797.2 4.1 copy.109
  804.0 2.2 copy.110
  807.4 5.6 convert_reduce_fusion.2
  814.0 37.7 %all-reduce.18 = (f32[512]{0:T(512)S(1)}, f32[512]{0:T(512)S(1)}, f32[512]{0:T(512)S(1)}, f32[512]{0:T(512)S(1)}, f32[512]{0:T(512)S(1)}, /*index=5*/f32[512]{0:...) all-reduce(f32[512]{0:T(512)S(1)} %get-tuple-element.18, ...), channel_id=2, replica_groups=mesh['dp'=32] {'dp'}, use_global_device_ids=true, to_apply=%region_12.13.clone | all-reduce | flops 8848 | bytes 70784
  858.7 2.8 fusion.39
  862.1 142.9 %reduce-scatter.11.cloned.1.call-done = f32[64,512]{1,0:T(8,128)} async-done(((f32[2048,512]{1,0:T(8,128)}), f32[64,512]{1,0:T(8,128)}) %reduce-scatter.11.cloned.1.call-update) | async-done | bytes 131088 | tf_op jit(solution)/shard_map/reduce_scatter | solution.py:305
  1004.9 139.8 %reduce-scatter.9.cloned.1.call-done = f32[16,2048]{1,0:T(8,128)} async-done(((f32[512,2048]{1,0:T(8,128)}), f32[16,2048]{1,0:T(8,128)}) %reduce-scatter.9.cloned.1.call-update) | async-done | bytes 131088 | tf_op jit(solution)/shard_map/reduce_scatter | solution.py:303
  (210 shorter events, 42.4 us)
Async XLA Ops:
  7.2 80.7 %copy-start = (bf16[169,16]{0,1:T(8,128)(2,1)S(1)}, bf16[169,16]{0,1:T(8,128)(2,1)}, u32[]{:S(2)}) copy-start(bf16[169,16]{0,1:T(8,128)(2,1)} %param.37) | copy-start | bytes 16228
  7.2 7.4 copy-start.18
  7.2 155.4 %all-gather.4.cloned.1.call-start = ((), (), s32[]{:S(2)}) async-start(), calls=%async_computation.4 | async-start | bytes 1622016 | tf_op jit(solution)/shard_map/all_gather | solution.py:104
  7.9 372.4 %all-gather.6.cloned.1.call-start = ((), (), s32[]{:S(2)}) async-start(), calls=%async_computation.5 | async-start | bytes 2162688 | tf_op jit(solution)/shard_map/all_gather | solution.py:111
  8.7 435.7 %all-gather.8.cloned.1.call-start = ((), (), s32[]{:S(2)}) async-start(), calls=%async_computation.6 | async-start | bytes 2162688 | tf_op jit(solution)/shard_map/all_gather | solution.py:113
  9.4 852.2 %reduce-scatter.7.cloned.1.call-start = ((), (), s32[]{:S(2)}) async-start(), calls=%async_computation.8 | async-start | bytes 1081344 | tf_op jit(solution)/shard_map/reduce_scatter | solution.py:299
  21.7 11.9 %copy-start.54 = (bf16[16]{0:T(256)(128)(2,1)S(1)}, bf16[16]{0:T(256)(128)(2,1)}, u32[]{:S(2)}) copy-start(bf16[16]{0:T(256)(128)(2,1)} %param.36) | copy-start | bytes 100
  21.8 64.3 %copy-start.30 = (s32[49,49]{1,0:T(8,128)S(1)}, s32[49,49]{1,0:T(8,128)}, u32[]{:S(2)}) copy-start(s32[49,49]{1,0:T(8,128)} %param.23) | copy-start | bytes 28816
  21.8 65.0 %copy-start.40 = (s32[14,14]{1,0:T(8,128)S(1)}, s32[14,14]{1,0:T(8,128)}, u32[]{:S(2)}) copy-start(s32[14,14]{1,0:T(8,128)} %param.22) | copy-start | bytes 2356
  27.7 64.4 %copy-start.31 = (bf16[16,512]{1,0:T(8,128)(2,1)S(1)}, bf16[16,512]{1,0:T(8,128)(2,1)}, u32[]{:S(2)}) copy-start(bf16[16,512]{1,0:T(8,128)(2,1)} %param.29) | copy-start | bytes 49156
  28.0 134.7 %copy-start.26 = (f32[3136]{0:T(1024)}, f32[3136]{0:T(1024)S(1)}, u32[]{:S(2)}) copy-start(f32[3136]{0:T(1024)S(1)} %div.27) | copy-start | bytes 37636
  32.8 106.8 %copy-start.8 = (bf16[16,11,14,512]{3,0,2,1:T(8,128)(2,1)S(1)}, bf16[16,11,14,512]{3,0,2,1:T(8,128)(2,1)}, u32[]{:S(2)}) copy-start(bf16[16,11,14,512]{3,0,2,1:T(8,128)(2,1)} %slice.82) | copy-start | bytes 7569412
  32.8 106.8 %copy-start.16 = (bf16[16,3,14,512]{3,0,2,1:T(8,128)(2,1)S(1)}, bf16[16,3,14,512]{3,0,2,1:T(8,128)(2,1)}, u32[]{:S(2)}) copy-start(bf16[16,3,14,512]{3,0,2,1:T(8,128)(2,1)} %slice.83) | copy-start | bytes 2064388
  33.6 53.4 %copy-start.41 = (f32[16]{0:T(128)}, f32[16]{0:T(128)S(1)}, u32[]{:S(2)}) copy-start(f32[16]{0:T(128)S(1)} %compare_convert_fusion) | copy-start | bytes 196
  146.6 7.9 copy-start.20
  154.5 8.1 copy-start.50
  154.5 8.1 copy-start.51
  154.5 8.2 copy-start.34
  154.5 8.2 copy-start.47
  154.7 18.8 %copy-start.28 = (f32[3136]{0:T(1024)}, f32[3136]{0:T(1024)S(1)}, u32[]{:S(2)}) copy-start(f32[3136]{0:T(1024)S(1)} %rsqrt.20) | copy-start | bytes 37636
  276.5 17.7 %copy-start.17 = (f32[16,49,49]{1,2,0:T(8,128)S(1)}, f32[16,49,49]{1,2,0:T(8,128)}, u32[]{:S(2)}) copy-start(f32[16,49,49]{1,2,0:T(8,128)} %copy.94) | copy-start | bytes 460996
  328.9 16.8 %copy-start.11 = (f32[16,4,16,49]{3,2,1,0:T(8,128)}, f32[16,4,16,49]{3,2,1,0:T(8,128)S(1)}, u32[]{:S(2)}) copy-start(f32[16,4,16,49]{3,2,1,0:T(8,128)S(1)} %log_add_fusion) | copy-start | bytes 602116
  370.1 6.3 copy-start.9
  370.1 10.3 copy-start.36
  370.1 10.3 copy-start.39
  370.1 10.3 copy-start.45
  376.3 2.7 copy-start.3
  376.3 106.9 %copy-start.21 = (f32[3136]{0:T(1024)}, f32[3136]{0:T(1024)S(1)}, u32[]{:S(2)}) copy-start(f32[3136]{0:T(1024)S(1)} %broadcast_multiply_fusion.5) | copy-start | bytes 37636
  380.3 102.9 %copy-start.24 = (f32[3136]{0:T(1024)}, f32[3136]{0:T(1024)S(1)}, u32[]{:S(2)}) copy-start(f32[3136]{0:T(1024)S(1)} %add_rsqrt_fusion.1) | copy-start | bytes 37636
  380.4 64.0 %copy-start.23 = (f32[3136]{0:T(1024)S(1)}, f32[3136]{0:T(1024)}, u32[]{:S(2)}) copy-start(f32[3136]{0:T(1024)} %mul.181) | copy-start | bytes 37636
  444.4 23.1 %copy-start.4 = (f32[3136,512]{1,0:T(8,128)S(1)}, f32[3136,512]{1,0:T(8,128)}, u32[]{:S(2)}) copy-start(f32[3136,512]{1,0:T(8,128)} %copy-done.3) | copy-start | bytes 19267588
  444.4 23.1 %copy-start.52 = (bf16[512,2048]{1,0:T(8,128)(2,1)S(1)}, bf16[512,2048]{1,0:T(8,128)(2,1)}, u32[]{:S(2)}) copy-start(bf16[512,2048]{1,0:T(8,128)(2,1)} %all-gather.6.cloned.1.call-done) | copy-start | bytes 6291460
  467.5 15.7 %copy-start.7 = (f32[3136,512]{1,0:T(8,128)S(1)}, f32[3136,512]{1,0:T(8,128)}, u32[]{:S(2)}) copy-start(f32[3136,512]{1,0:T(8,128)} %reshape.206) | copy-start | bytes 19267588
  483.2 10.0 copy-start.10
  511.9 17.7 %copy-start.12 = (f32[16,4,16,49]{3,2,1,0:T(8,128)S(1)}, f32[16,4,16,49]{3,2,1,0:T(8,128)}, u32[]{:S(2)}) copy-start(f32[16,4,16,49]{3,2,1,0:T(8,128)} %copy-done.11) | copy-start | bytes 602116
  626.2 235.8 %reduce-scatter.5.cloned.1.call-start = ((), (), s32[]{:S(2)}) async-start(), calls=%async_computation.7 | async-start | bytes 3244032 | tf_op jit(solution)/shard_map/reduce_scatter | solution.py:296
  676.0 3.1 copy-start.13
  693.2 14.2 %copy-start.27 = (f32[3136]{0:T(1024)S(1)}, f32[3136]{0:T(1024)}, u32[]{:S(2)}) copy-start(f32[3136]{0:T(1024)} %copy-done.26) | copy-start | bytes 37636
  693.2 14.2 %copy-start.29 = (f32[3136]{0:T(1024)S(1)}, f32[3136]{0:T(1024)}, u32[]{:S(2)}) copy-start(f32[3136]{0:T(1024)} %copy-done.28) | copy-start | bytes 37636
  693.2 14.2 %copy-start.35 = (f32[512]{0:T(512)S(1)}, f32[512]{0:T(512)}, u32[]{:S(2)}) copy-start(f32[512]{0:T(512)} %convert_element_type.159) | copy-start | bytes 6148
  693.2 14.2 %copy-start.48 = (f32[512]{0:T(512)S(1)}, f32[512]{0:T(512)}, u32[]{:S(2)}) copy-start(f32[512]{0:T(512)} %convert_element_type.160) | copy-start | bytes 6148
  721.3 283.6 %reduce-scatter.11.cloned.1.call-start = ((), (), s32[]{:S(2)}) async-start(), calls=%async_computation.10 | async-start | bytes 4325376 | tf_op jit(solution)/shard_map/reduce_scatter | solution.py:305
  721.3 14.1 %copy-start.22 = (f32[3136]{0:T(1024)S(1)}, f32[3136]{0:T(1024)}, u32[]{:S(2)}) copy-start(f32[3136]{0:T(1024)} %copy-done.21) | copy-start | bytes 37636
  721.3 14.1 %copy-start.25 = (f32[3136]{0:T(1024)S(1)}, f32[3136]{0:T(1024)}, u32[]{:S(2)}) copy-start(f32[3136]{0:T(1024)} %copy-done.24) | copy-start | bytes 37636
  721.4 14.1 %copy-start.37 = (f32[512]{0:T(512)S(1)}, f32[512]{0:T(512)}, u32[]{:S(2)}) copy-start(f32[512]{0:T(512)} %convert_element_type.168) | copy-start | bytes 6148
  721.4 14.1 %copy-start.46 = (f32[512]{0:T(512)S(1)}, f32[512]{0:T(512)}, u32[]{:S(2)}) copy-start(f32[512]{0:T(512)} %convert_element_type.169) | copy-start | bytes 6148
  735.0 16.9 %copy-start.49 = (bf16[512]{0:T(512)(128)(2,1)S(1)}, bf16[512]{0:T(512)(128)(2,1)}, u32[]{:S(2)}) copy-start(bf16[512]{0:T(512)(128)(2,1)} %get-tuple-element.42) | copy-start | bytes 3076
  735.0 16.9 %copy-start.6 = (bf16[16,14,14,512]{3,0,2,1:T(8,128)(2,1)S(1)}, bf16[16,14,14,512]{3,0,2,1:T(8,128)(2,1)}, u32[]{:S(2)}) copy-start(bf16[16,14,14,512]{3,0,2,1:T(8,128)(2,1)} %copy-done.5) | copy-start | bytes 9633796
  735.0 16.9 %copy-start.42 = (f32[16]{0:T(128)S(1)}, f32[16]{0:T(128)}, u32[]{:S(2)}) copy-start(f32[16]{0:T(128)} %copy-done.41) | copy-start | bytes 196
  735.0 409.8 %reduce-scatter.9.cloned.1.call-start = ((), (), s32[]{:S(2)}) async-start(), calls=%async_computation.9 | async-start | bytes 4325376 | tf_op jit(solution)/shard_map/reduce_scatter | solution.py:303
  767.7 6.9 slice-start.2
  767.7 6.9 copy-start.53
  767.7 6.9 slice-start.3
  772.9 16.3 %slice-start = ((s8[6422528]{0:T(1024)(128)(4,1)}), s8[4194304]{0:T(1024)(128)(4,1)S(1)}, s32[]{:S(2)}) async-start(s8[6422528]{0:T(1024)(128)(4,1)} %bitcast.95), calls=%async_computation.11 | async-start | bytes 8388608
  774.6 14.6 %slice-start.1 = ((s8[6422528]{0:T(1024)(128)(4,1)}), s8[2228224]{0:T(1024)(128)(4,1)S(1)}, s32[]{:S(2)}) async-start(s8[6422528]{0:T(1024)(128)(4,1)} %bitcast.95), calls=%async_computation.12 | async-start | bytes 4456448
  802.2 10.8 copy-start.32
  802.2 11.7 %copy-start.33 = (f32[512]{0:T(512)S(1)}, f32[512]{0:T(512)}, u32[]{:S(2)}) copy-start(f32[512]{0:T(512)} %get-tuple-element.45) | copy-start | bytes 6148
  802.2 11.7 %copy-start.38 = (f32[2048]{0:T(1024)S(1)}, f32[2048]{0:T(1024)}, u32[]{:S(2)}) copy-start(f32[2048]{0:T(1024)} %get-tuple-element.62) | copy-start | bytes 24580
  802.3 11.7 %copy-start.43 = (f32[512]{0:T(512)S(1)}, f32[512]{0:T(512)}, u32[]{:S(2)}) copy-start(f32[512]{0:T(512)} %get-tuple-element.16) | copy-start | bytes 6148
  802.3 11.7 %copy-start.44 = (f32[512]{0:T(512)S(1)}, f32[512]{0:T(512)}, u32[]{:S(2)}) copy-start(f32[512]{0:T(512)} %get-tuple-element.22) | copy-start | bytes 6148
  804.0 52.9 %copy-start.14 = (bf16[16,11,14,512]{3,0,2,1:T(8,128)(2,1)S(1)}, bf16[16,11,14,512]{3,0,2,1:T(8,128)(2,1)}, u32[]{:S(2)}) copy-start(bf16[16,11,14,512]{3,0,2,1:T(8,128)(2,1)} %slice.98) | copy-start | bytes 7569412
  804.0 52.9 %copy-start.19 = (bf16[16,3,14,512]{3,0,2,1:T(8,128)(2,1)S(1)}, bf16[16,3,14,512]{3,0,2,1:T(8,128)(2,1)}, u32[]{:S(2)}) copy-start(bf16[16,3,14,512]{3,0,2,1:T(8,128)(2,1)} %slice.97) | copy-start | bytes 2064388
  807.4 337.4 %copy-start.1 = (bf16[169,16]{0,1:T(8,128)(2,1)S(1)}, bf16[169,16]{0,1:T(8,128)(2,1)}, u32[]{:S(2)}) copy-start(bf16[169,16]{0,1:T(8,128)(2,1)} %param.37) | copy-start | bytes 16228
  851.6 7.1 copy-start.15
  (2 other events, 4.4 us)
Sparse Core Ops, SparseCore 0:
  10.9 57.8 all-gather.3
  71.7 55.8 all-gather.5
  130.5 55.4 all-gather.7
  626.4 130.8 reduce-scatter.6
  764.0 97.9 reduce-scatter.4
  864.9 140.0 reduce-scatter.10
  1007.9 136.8 reduce-scatter.8
where the time goes:
time: 1170 us; the launch traced here: 1150 us
  local copies, waits for them, and re-layouts  334 us (29%)
  matrix products  305 us (26%)
  waiting for transfers between devices  285 us (24%)
  blocking collectives  126 us (11%)
  other arithmetic  84.7 us (7%)
  between operations  16 us (1%)
    reduce_scatter x1, waiting for transfers between devices, local(): lax.psum_scatter(grad_out_weight, 'dp', scatter_dimension=0, tiled=True)  143 us
    reduce_scatter x1, waiting for transfers between devices, local(): lax.psum_scatter(grad_hidden_weight, 'dp', scatter_dimension=0, tiled=True)  140 us
    unnamed x2, blocking collectives  80.3 us
    unnamed x151, local copies, waits for them, and re-layouts  77.6 us
    dot_general x1, matrix products, local(): jnp.dot(second_in, hidden_full, preferred_element_type=jnp.float32)  64 us
    dot_general x4, matrix products, transposed_dot(): lax.dot_general(left, right, (((0,), (0,)), ((), ())), preferred_element_...  46.6 us
    all_gather x1, blocking collectives, local(): lax.all_gather(proj_weight, 'dp', axis=0, tiled=True)  45.6 us
    reshape x1, local copies, waits for them, and re-layouts, local(): windows = qkv_rows.reshape(images, window_count, span, 3, heads, head_size)  41.9 us
  transfers between devices with their start and end apart: 7, of which 3 were waited for; matrix products, arithmetic and copies ran while one was open for 47% of the time, Pallas kernels for 0%

commit v1 on v0

v1 whole, which is shorter than its diff:
```python
import functools
import math

import jax
import jax.numpy as jnp
from jax import lax
from jax.experimental import pallas as pl
from jax.experimental.pallas import tpu as pltpu
from jax.sharding import PartitionSpec as P

WIN = 7
MAP = 14
SHIFT = 3
SPAN = WIN * WIN
PAD = 64
GROUP = 2
EPS = 1e-05
MASK_FILL = -100.0
NEG = -1e30
F32 = jnp.float32
BF16 = jnp.bfloat16


def to_windows(field):
    images = field.shape[0]
    count = MAP // WIN
    rolled = jnp.roll(field, (-SHIFT, -SHIFT), axis=(1, 2))
    blocks = rolled.reshape(images, count, WIN, count, WIN, field.shape[-1])
    blocks = blocks.transpose(0, 1, 3, 2, 4, 5).reshape(
        images, count * count, SPAN, field.shape[-1]
    )
    blocks = jnp.pad(blocks, ((0, 0), (0, 0), (0, PAD - SPAN), (0, 0)))
    return blocks.reshape(images, count * count * PAD, field.shape[-1])


def from_windows(blocks):
    images = blocks.shape[0]
    count = MAP // WIN
    blocks = blocks.reshape(images, count * count, PAD, blocks.shape[-1])[:, :, :SPAN]
    grid = blocks.reshape(images, count, count, WIN, WIN, blocks.shape[-1])
    grid = grid.transpose(0, 1, 3, 2, 4, 5).reshape(images, MAP, MAP, blocks.shape[-1])
    return jnp.roll(grid, (SHIFT, SHIFT), axis=(1, 2))


def nn(a, b):
    return jnp.dot(a, b, preferred_element_type=F32)


def nt(a, b):
    return lax.dot_general(a, b, (((1,), (1,)), ((), ())), preferred_element_type=F32)


def tn(a, b):
    return lax.dot_general(a, b, (((0,), (0,)), ((), ())), preferred_element_type=F32)


def row_mean(values):
    return jnp.mean(values, axis=-1, keepdims=True)


def block_kernel(
    counts,
    x_ref,
    c_ref,
    w_ref,
    v_ref,
    bias_ref,
    act_ref,
    tg_ref,
    gw_ref,
    gv_ref,
    gs_ref,
    acc,
    p_s,
    qkv_s,
    mixed_s,
    gm_s,
    gqkv_s,
    first_s,
    n1_s,
    *,
    scale,
):
    step = pl.program_id(0)
    rows = x_ref.shape[0] * x_ref.shape[1]
    per_image = x_ref.shape[1]
    width = x_ref.shape[2]
    lane = lax.broadcasted_iota(jnp.int32, (1, 128), 1) // 32
    lane_masks = [lane == h for h in range(4)]
    zero_low = jnp.zeros((), BF16)

    @pl.when(step == 0)
    def _():
        acc[...] = jnp.zeros_like(acc)
        gv_ref[...] = jnp.zeros_like(gv_ref)
        gs_ref[...] = jnp.zeros_like(gs_ref)

    def vec(i):
        return v_ref[i : i + 1, :]

    def stacked(a):
        return jnp.concatenate([jnp.where(m, a, zero_low) for m in lane_masks], axis=0)

    def unstacked(a):
        total = jnp.where(lane_masks[0], a[0:128], 0.0)
        for h in range(1, 4):
            total = jnp.where(lane_masks[h], a[128 * h : 128 * (h + 1)], total)
        return total

    ones = jnp.ones((8, rows), BF16)

    def add_vec(i, total):
        gv_ref[i : i + 1, :] += total

    def low_total(a):
        return nn(ones, a)[0:1]

    x = x_ref[...].reshape(rows, width).astype(F32)
    centred = x - row_mean(x)
    r1 = lax.rsqrt(row_mean(centred * centred) + EPS)
    n1 = centred * r1
    n1_s[...] = n1
    first = (n1 * vec(0) + vec(1)).astype(BF16)
    first_s[...] = first
    qkv_s[:, 0:width] = (nn(first, w_ref[0]) + vec(2)).astype(BF16)
    qkv_s[:, width : 2 * width] = nn(first, w_ref[1]).astype(BF16)
    qkv_s[:, 2 * width : 3 * width] = (nn(first, w_ref[2]) + vec(3)).astype(BF16)

    def forward_pair(pr, carry):
        at = pl.ds(pl.multiple_of(pr * 128, 128), 128)
        pair = lax.rem(pr, 2)
        for g in range(4):
            q = qkv_s[at, 128 * g : 128 * (g + 1)]
            k = qkv_s[at, width + 128 * g : width + 128 * (g + 1)]
            v = qkv_s[at, 2 * width + 128 * g : 2 * width + 128 * (g + 1)]
            s = nt(stacked(k), q) * scale + bias_ref[pair, g]
            s = s.reshape(4, 128, 128)
            e = jnp.exp(s - jnp.max(s, axis=1, keepdims=True))
            p = e * (1.0 / jnp.sum(e, axis=1, keepdims=True))
            p = p.reshape(512, 128)
            p_s[pr, g] = p
            mixed_s[at, 128 * g : 128 * (g + 1)] = tn(p.astype(BF16), stacked(v)).astype(BF16)
        return carry

    lax.fori_loop(0, rows // 128, forward_pair, 0)

    after = x + nn(mixed_s[...], w_ref[3]) + vec(4)
    centred = after - row_mean(after)
    r2 = lax.rsqrt(row_mean(centred * centred) + EPS)
    n2 = centred * r2
    second = (n2 * vec(5) + vec(6)).astype(BF16)
    image = step * GROUP + lax.broadcasted_iota(jnp.int32, (rows, 1), 0) // per_image
    valid = image < counts[0]
    go = jnp.where(valid, c_ref[...].reshape(rows, width).astype(F32), 0.0)
    gob = go.astype(BF16)
    add_vec(7, low_total(gob))
    outcome = after + vec(7)
    e2 = None
    for j in range(4):
        hidden = nn(second, w_ref[4 + j]) + vec(8 + j)
        cumulative = 0.5 * (1.0 + lax.erf(hidden * (1.0 / math.sqrt(2.0))))
        density = jnp.exp(-0.5 * hidden * hidden) * (1.0 / math.sqrt(2.0 * math.pi))
        active = (hidden * cumulative).astype(BF16)
        slope = cumulative + hidden * density
        outcome = outcome + nn(active, w_ref[8 + j])
        gh = (nt(gob, w_ref[8 + j]) * slope).astype(BF16)
        acc[8 + j] += tn(active, gob)
        acc[4 + j] += tn(second, gh)
        add_vec(8 + j, low_total(gh))
        part = nt(gh, w_ref[4 + j])
        e2 = part if e2 is None else e2 + part
    act_ref[...] = jnp.where(valid, outcome, 0.0).astype(BF16).reshape(act_ref.shape)
    add_vec(5, jnp.sum(e2 * n2, axis=0, keepdims=True))
    add_vec(6, jnp.sum(e2, axis=0, keepdims=True))
    f = e2 * vec(5)
    grad_after = go + r2 * (f - row_mean(f) - n2 * row_mean(f * n2))
    gp = grad_after.astype(BF16)
    acc[3] += tn(mixed_s[...], gp)
    add_vec(4, low_total(gp))
    gm_s[...] = nt(gp, w_ref[3]).astype(BF16)

    def backward_pair(pr, carry):
        at = pl.ds(pl.multiple_of(pr * 128, 128), 128)
        for g in range(4):
            q = qkv_s[at, 128 * g : 128 * (g + 1)]
            k = qkv_s[at, width + 128 * g : width + 128 * (g + 1)]
            v = qkv_s[at, 2 * width + 128 * g : 2 * width + 128 * (g + 1)]
            gm = gm_s[at, 128 * g : 128 * (g + 1)]
            p = p_s[pr, g]
            dp = nt(stacked(v), gm)
            dv = unstacked(nn(p.astype(BF16), gm))
            inner = jnp.sum((p * dp).reshape(4, 128, 128), axis=1, keepdims=True)
            ds = (p.reshape(4, 128, 128) * (dp.reshape(4, 128, 128) - inner)).reshape(512, 128)
            dsb = ds.astype(BF16)
            gs_ref[g] += dsb.astype(F32)
            dk = unstacked(nn(dsb, q)) * scale
            dq = tn(dsb, stacked(k)) * scale
            gqkv_s[at, 128 * g : 128 * (g + 1)] = dq.astype(BF16)
            gqkv_s[at, width + 128 * g : width + 128 * (g + 1)] = dk.astype(BF16)
            gqkv_s[at, 2 * width + 128 * g : 2 * width + 128 * (g + 1)] = dv.astype(BF16)
        return carry

    lax.fori_loop(0, rows // 128, backward_pair, 0)

    first = first_s[...]
    e1 = None
    for j in range(3):
        gq = gqkv_s[:, width * j : width * (j + 1)]
        acc[j] += tn(first, gq)
        part = nt(gq, w_ref[j])
        e1 = part if e1 is None else e1 + part
        if j == 0:
            add_vec(2, low_total(gq))
        if j == 2:
            add_vec(3, low_total(gq))
    n1 = n1_s[...]
    add_vec(0, jnp.sum(e1 * n1, axis=0, keepdims=True))
    add_vec(1, jnp.sum(e1, axis=0, keepdims=True))
    f = e1 * vec(0)
    grad_in = grad_after + r1 * (f - row_mean(f) - n1 * row_mean(f * n1))
    tg_ref[...] = grad_in.astype(BF16).reshape(tg_ref.shape)

    @pl.when(step == pl.num_programs(0) - 1)
    def _():
        for j in range(12):
            gw_ref[j] = acc[j].astype(BF16)


def run_block(counts, x, c, weights, vectors, bias, scale):
    images, per_image, width = x.shape
    rows = GROUP * per_image
    whole = functools.partial(pl.BlockSpec, pipeline_mode=pl.Buffered(1))
    tile = pl.BlockSpec((GROUP, per_image, width), lambda i: (i, 0, 0))
    return pl.pallas_call(
        functools.partial(block_kernel, scale=scale),
        grid=(images // GROUP,),
        in_specs=[
            pl.BlockSpec(memory_space=pltpu.SMEM),
            tile,
            tile,
            whole(weights.shape, lambda i: (0, 0, 0)),
            whole(vectors.shape, lambda i: (0, 0)),
            whole(bias.shape, lambda i: (0, 0, 0, 0)),
        ],
        out_specs=[
            tile,
            tile,
            whole(weights.shape, lambda i: (0, 0, 0)),
            pl.BlockSpec(vectors.shape, lambda i: (0, 0)),
            pl.BlockSpec((4, 512, 128), lambda i: (0, 0, 0)),
        ],
        out_shape=[
            jax.ShapeDtypeStruct(x.shape, BF16),
            jax.ShapeDtypeStruct(x.shape, BF16),
            jax.ShapeDtypeStruct(weights.shape, BF16),
            jax.ShapeDtypeStruct(vectors.shape, F32),
            jax.ShapeDtypeStruct((4, 512, 128), F32),
        ],
        scratch_shapes=[
            pltpu.VMEM(weights.shape, F32),
            pltpu.VMEM((rows // 128, 4, 512, 128), F32),
            pltpu.VMEM((rows, 3 * width), BF16),
            pltpu.VMEM((rows, width), BF16),
            pltpu.VMEM((rows, width), BF16),
            pltpu.VMEM((rows, 3 * width), BF16),
            pltpu.VMEM((rows, width), BF16),
            pltpu.VMEM((rows, width), F32),
        ],
        compiler_params=pltpu.CompilerParams(
            dimension_semantics=("arbitrary",), vmem_limit_bytes=60 * 1024 * 1024
        ),
    )(counts, x, c, weights, vectors, bias)


def bit_orders(count):
    bits = count.bit_length() - 1
    far = list(range(bits - 1, 0, -1))
    orders = []
    for turn in range(3):
        cut = (turn * len(far)) // 3
        orders.append(far[cut:] + far[:cut] + [0])
    return orders


def swap(array, bit, count):
    return lax.ppermute(array, "dp", [(i, i ^ (1 << bit)) for i in range(count)])


def gather_all(block, order, count, me):
    buffer = block
    for level, bit in enumerate(order):
        other = swap(buffer, bit, count)
        high = ((me >> bit) & 1) == 1
        buffer = jnp.stack(
            [jnp.where(high, other, buffer), jnp.where(high, buffer, other)], axis=level
        )
    bits = len(order)
    back = [order.index(b) for b in range(bits - 1, -1, -1)]
    buffer = buffer.transpose(*back, *range(bits, bits + block.ndim))
    return buffer.reshape(count, *block.shape)


def scatter_sum(blocks, order, count, me):
    bits = len(order)
    buffer = blocks.reshape(*([2] * bits), *blocks.shape[1:])
    left = list(range(bits - 1, -1, -1))
    for bit in order:
        axis = left.index(bit)
        mine = (me >> bit) & 1
        keep = lax.dynamic_index_in_dim(buffer, mine, axis, keepdims=False)
        send = lax.dynamic_index_in_dim(buffer, 1 - mine, axis, keepdims=False)
        got = swap(send, bit, count)
        buffer = (keep.astype(F32) + got.astype(F32)).astype(BF16)
        left.remove(bit)
    return buffer


def local(
    tokens,
    cotangent,
    counts,
    region_ids,
    relative_index,
    attn_gain,
    attn_shift,
    qkv_weight,
    query_bias,
    value_bias,
    proj_weight,
    proj_bias,
    mlp_gain,
    mlp_shift,
    hidden_weight,
    hidden_bias,
    output_weight,
    output_bias,
    bias_table,
    *,
    count,
):
    me = lax.axis_index("dp")
    width = tokens.shape[-1]
    heads = bias_table.shape[1]
    table_rows = bias_table.shape[0]
    scale = (width // heads) ** (-0.5)
    share = qkv_weight.shape[0]
    wide = hidden_bias.shape[0]
    orders = bit_orders(count)

    small = jnp.concatenate(
        [
            attn_gain,
            attn_shift,
            query_bias,
            value_bias,
            proj_bias,
            mlp_gain,
            mlp_shift,
            output_bias,
            hidden_bias,
        ]
    )
    small_len = small.shape[0]
    small = jnp.pad(small, (0, width - small_len)).reshape(1, width)
    pack_one = jnp.concatenate(
        [qkv_weight[:, width * j : width * (j + 1)] for j in range(3)] + [proj_weight], axis=0
    )
    pack_two = jnp.concatenate(
        [hidden_weight[:, width * j : width * (j + 1)] for j in range(4)] + [small], axis=0
    )
    got_one = gather_all(pack_one, orders[0], count, me)
    got_two = gather_all(pack_two, orders[1], count, me)
    got_three = gather_all(output_weight, orders[2], count, me)

    def joined(got):
        return got[:, : 4 * share].reshape(count, 4, share, width).transpose(1, 0, 2, 3).reshape(
            4, width, width
        )

    weights = jnp.concatenate(
        [joined(got_one), joined(got_two), got_three.reshape(4, width, width)], axis=0
    )
    got_small = got_two[:, 4 * share, :small_len].astype(F32)
    vectors = jnp.concatenate(
        [
            got_small[:, : 8 * share].reshape(count, 8, share).transpose(1, 0, 2).reshape(8, width),
            got_small[:, 8 * share :].reshape(4, width),
            jnp.zeros((4, width), F32),
        ],
        axis=0,
    )

    n_win = (MAP // WIN) ** 2
    cells = (
        region_ids.reshape(MAP // WIN, WIN, MAP // WIN, WIN)
        .transpose(0, 2, 1, 3)
        .reshape(n_win, SPAN)
    )
    mask = jnp.where(cells[:, :, None] == cells[:, None, :], 0.0, MASK_FILL).astype(F32)
    mask = jnp.pad(mask, ((0, 0), (0, 0), (0, PAD - SPAN)))
    mask = jnp.pad(mask, ((0, 0), (0, PAD - SPAN), (0, 0)), constant_values=NEG)
    by_key = relative_index.T
    padded_index = jnp.pad(by_key, ((0, PAD - SPAN), (0, PAD - SPAN)), constant_values=-1)
    hot = (jnp.arange(table_rows)[:, None] == padded_index.reshape(1, -1)).astype(BF16)
    position = tn(bias_table, hot).reshape(heads, PAD, PAD)
    per_window = position[None] + mask[:, None]
    per_pair = per_window.reshape(n_win // 2, 2, heads, PAD, PAD)
    off = jnp.full((n_win // 2, heads, PAD, PAD), NEG, F32)
    bias = jnp.concatenate(
        [
            jnp.concatenate([per_pair[:, 0], off], axis=-1),
            jnp.concatenate([off, per_pair[:, 1]], axis=-1),
        ],
        axis=-2,
    ).reshape(n_win // 2, 4, 512, 128)

    act, tg, gw, gv, gs = run_block(
        counts, to_windows(tokens), to_windows(cotangent), weights, vectors, bias, scale
    )

    def cut(four):
        return four.reshape(4, count, share, width).transpose(1, 0, 2, 3).reshape(
            count, 4 * share, width
        )

    small_grad = jnp.concatenate(
        [
            gv[:8].reshape(8, count, share).transpose(1, 0, 2).reshape(count, 8 * share),
            gv[8:12].reshape(count, wide),
        ],
        axis=1,
    ).astype(BF16)
    small_grad = jnp.pad(small_grad, ((0, 0), (0, width - small_len)))[:, None]
    own_one = scatter_sum(cut(gw[0:4]), orders[0][::-1], count, me).astype(F32)
    own_two = scatter_sum(
        jnp.concatenate([cut(gw[4:8]), small_grad], axis=1), orders[1][::-1], count, me
    ).astype(F32)
    own_three = scatter_sum(
        gw[8:12].reshape(count, 4 * share, width), orders[2][::-1], count, me
    ).astype(F32)

    gs = gs.reshape(heads, 128, 128)
    gs = gs[:, :SPAN, :SPAN] + gs[:, PAD : PAD + SPAN, PAD : PAD + SPAN]
    hot_back = (by_key.reshape(-1, 1) == jnp.arange(table_rows)[None, :]).astype(F32)
    table = jnp.dot(
        gs.reshape(heads, SPAN * SPAN),
        hot_back,
        precision=lax.Precision.HIGHEST,
        preferred_element_type=F32,
    )
    for bit in orders[0][::-1]:
        table = table + swap(table, bit, count)

    own_small = own_two[4 * share]

    def piece(i):
        return own_small[i * share : (i + 1) * share]

    return (
        from_windows(act),
        from_windows(tg),
        piece(0),
        piece(1),
        jnp.concatenate([own_one[share * j : share * (j + 1)] for j in range(3)], axis=1),
        piece(2),
        piece(3),
        own_one[3 * share :],
        piece(4),
        piece(5),
        piece(6),
        jnp.concatenate([own_two[share * j : share * (j + 1)] for j in range(4)], axis=1),
        own_small[8 * share : 8 * share + wide],
        own_three,
        piece(7),
        table.T,
    )


def solution(mesh):
    row = P("dp")
    matrix = P("dp", None)
    field = P("dp", None, None, None)
    return jax.shard_map(
        functools.partial(local, count=mesh.shape["dp"]),
        mesh=mesh,
        in_specs=(
            field,
            field,
            row,
            P(),
            P(),
            row,
            row,
            matrix,
            row,
            row,
            matrix,
            row,
            row,
            row,
            matrix,
            row,
            matrix,
            row,
            P(),
        ),
        out_specs=(
            field,
            field,
            row,
            row,
            matrix,
            row,
            row,
            matrix,
            row,
            row,
            row,
            matrix,
            row,
            matrix,
            row,
            P(),
        ),
        check_vma=False,
    )
```

time: 1170 us -> 410 us (0.35); the launches traced: 1150 us -> 404 us
  matrix products: 305 us -> 2.91 us
  local copies, waits for them, and re-layouts: 334 us -> 80.3 us
  waiting for transfers between devices: 285 us -> 68.8 us
  Pallas kernels: 0 us -> 183 us
  blocking collectives: 126 us -> 0 us
  other arithmetic: 84.7 us -> 37.3 us
  starting transfers between devices: 0.68 us -> 29.4 us
  between operations: 16 us -> 2.53 us
    dot_general x20 -> x2, matrix products: 305 us -> 2.91 us  [the longest x1 2.01 us: tn(): lax.dot_general(a, b, (((0,), (0,)), ((), ())), preferred_element_type=F32)]
    reduce_scatter x4 -> x0, waiting for transfers between devices: 283 us -> none  [the longest x1 143 us: local(): lax.psum_scatter(grad_out_weight, 'dp', scatter_dimension=0, tiled=True)]
    pallas_call x0 -> x1, Pallas kernels: none -> 183 us  [run_block(): pl.pallas_call(functools.partial(block_kernel, scale=scale), grid=(images...]
    convert_element_type x11 -> x0, local copies, waits for them, and re-layouts: 112 us -> none  [the longest x2 25.5 us: local(): grad_keys.reshape(-1, width).astype(jnp.bfloat16)]
    unnamed x2 -> x0, blocking collectives: 80.3 us -> none
    reshape x8 -> x12, local copies, waits for them, and re-layouts: 85 us -> 8.23 us  [the longest x1 4.6 us: gather_all(): return buffer.reshape(count, *block.shape)]
    ppermute x0 -> x35, waiting for transfers between devices: none -> 68.8 us  [swap(): return lax.ppermute(array, 'dp', [(i, i ^ 1 << bit) for i in range(count)])]
    reduce_sum x8 -> x0, other arithmetic: 68.3 us -> none  [the longest x1 27.3 us: local(): grad_position = jnp.sum(grad_scores, axis=(0, 1), dtype=jnp.float32)]
  transfers between devices with their start and end apart: 7 -> 35, of which waited for: 3 -> 18; matrix products, arithmetic and copies ran while one was open for 47% -> 22% of each run, Pallas kernels for 0% -> 0%
where the time goes in v1:
time: 410 us; the launch traced here: 404 us
  Pallas kernels  183 us (45%)
  local copies, waits for them, and re-layouts  80.3 us (20%)
  waiting for transfers between devices  68.8 us (17%)
  other arithmetic  37.3 us (9%)
  starting transfers between devices  29.4 us (7%)
    pallas_call x1, Pallas kernels, run_block(): pl.pallas_call(functools.partial(block_kernel, scale=scale), grid=(images...  183 us
    ppermute x35, waiting for transfers between devices, swap(): return lax.ppermute(array, 'dp', [(i, i ^ 1 << bit) for i in range(count)])  68.8 us
    ppermute x35, starting transfers between devices, swap(): return lax.ppermute(array, 'dp', [(i, i ^ 1 << bit) for i in range(count)])  29.4 us
    unnamed x77, local copies, waits for them, and re-layouts  16.5 us
    another operation x28, other arithmetic, gather_all(): jnp.stack([jnp.where(high, other, buffer), jnp.where(high, buffer, other)...  10.1 us
  transfers between devices with their start and end apart: 35, of which 18 were waited for; matrix products, arithmetic and copies ran while one was open for 22% of the time, Pallas kernels for 0%

profile of v1, /device:TPU:0, one launch (start us, length us, event | category | flops | bytes accessed | tf_op | source)
XLA Modules:
  0.0 403.9 jit_solution(10296987150034532560)
XLA Ops:
  1.4 1.4 pad_maximum_fusion.22
  2.8 4.0 collective-permute-start
  6.8 1.5 collective-permute-start.10
  11.2 6.1 %concatenate.75 = bf16[192]{0:T(256)(128)(2,1)S(1)} concatenate(bf16[16]{0:T(256)(128)(2,1)} %param.24, bf16[16]{0:T(256)(128)(2,1)} %param.25, bf16[16]{0:T(256)(128)(2,1)} %param.27, bf16[16]{0:T(256)(128)(2,1)} %param.28, bf16[16]{0:T(256)(128)(2,1)} %param.30, bf16[16]{0:T(256)(128)(2,1)} %param.31, bf16[16]{0:T(256)(128)(2,1)} %param.32, bf16[16]{0:T(256)(128)(2,1)} %param.36, ...), dimensions={0} | concatenate | bytes 768 | tf_op jit(solution)/shard_map/concatenate | solution.py:350
  17.3 1.6 collective-permute-start.5
  20.1 2.1 slice.212
  23.7 1.7 slice.216
  26.5 2.0 convolution_bitcast_fusion
  28.5 1.9 add.166
  30.4 1.3 broadcast_add_fusion
  31.7 1.4 slice_bitcast_fusion.1
  34.5 1.8 fusion.2
  36.4 1.7 fusion.5
  40.4 1.6 collective-permute-start.11
  45.9 3.8 collective-permute-done.6
  50.4 2.3 collective-permute-done.2
  53.4 4.7 %collective-permute-done.12 = bf16[2,2,64,512]{3,2,1,0:T(8,128)(2,1)S(1)} collective-permute-done((bf16[2,2,64,512]{3,2,1,0:T(8,128)(2,1)S(1)}, bf16[2,2,64,512]{3,2,1,0:T(8,128)(2,1)S(1)}, u32[]{:S(2)}, u32[]{:S(2)}) %collective-permute-start.12) | collective-permute-done | bytes 262176 | tf_op jit(solution)/shard_map/ppermute | solution.py:286
  58.3 1.3 collective-permute-done.7
  60.5 1.3 copy.246
  62.1 5.3 %collective-permute-done.3 = bf16[2,2,2,64,512]{4,3,2,1,0:T(8,128)(2,1)S(1)} collective-permute-done((bf16[2,2,2,64,512]{4,3,2,1,0:T(8,128)(2,1)S(1)}, bf16[2,2,2,64,512]{4,3,2,1,0:T(8,128)(2,1)S(1)}, u32[]{:S(2)}, u32[]{:S(2)}) %collective-permute-start.3) | collective-permute-done | bytes 524320 | tf_op jit(solution)/shard_map/ppermute | solution.py:286
  68.7 10.3 %collective-permute-done.13 = bf16[2,2,2,64,512]{4,3,2,1,0:T(8,128)(2,1)S(1)} collective-permute-done((bf16[2,2,2,64,512]{4,3,2,1,0:T(8,128)(2,1)S(1)}, bf16[2,2,2,64,512]{4,3,2,1,0:T(8,128)(2,1)S(1)}, u32[]{:S(2)}, u32[]{:S(2)}) %collective-permute-start.13) | collective-permute-done | bytes 524320 | tf_op jit(solution)/shard_map/ppermute | solution.py:286
  81.2 2.0 fusion.3
  84.0 2.2 copy.235
  86.2 1.8 copy.285
  88.1 2.7 pad.30.clone
  91.2 1.8 copy.284
  93.1 2.7 pad.29.clone
  98.8 1.7 select_maximum_fusion
  100.5 1.4 select_bitcast_fusion.5
  102.1 1.5 copy.241
  103.7 1.4 select_bitcast_fusion.3
  105.2 1.5 copy.257
  107.3 3.6 copy.252
  110.8 4.6 %reshape.188 = bf16[32,65,512]{2,0,1:T(8,128)(2,1)S(1)} reshape(bf16[2,2,2,2,2,65,512]{6,4,3,2,1,0,5:T(2,128)(2,1)} %copy.252) | data formatting | bytes 4259840 | tf_op jit(solution)/shard_map/reshape | solution.py:300
  115.6 2.5 copy.253
  118.5 5.5 %pad_maximum_fusion.w_ref = bf16[12,512,512]{2,1,0:T(8,128)(2,1)} fusion(bf16[4,512,512]{2,1,0:T(8,128)(2,1)} %bitcast.267, bf16[4,512,512]{2,1,0:T(8,128)(2,1)} %bitcast.268, bf16[4,512,512]{2,1,0:T(8,128)(2,1)S(1)} %bitcast.266), kind=kLoop, calls=%fused_computation | loop fusion | flops 6291456 | bytes 12582912 | tf_op jit(solution)/shard_map/concatenate | solution.py:380
  124.7 182.7 %shard_map.306 = (bf16[16,256,512]{2,1,0:T(8,128)(2,1)}, bf16[16,256,512]{2,1,0:T(8,128)(2,1)}, bf16[12,512,512]{2,1,0:T(8,128)(2,1)}, f32[16,512]{1,0:T(8,128)}, f32[4,512,128]{2,1,0:T(8,128)}) custom-call(s32[1]{0:T(128)S(6)} %copy.310.counts, bf16[16,256,512]{2,1,0:T(8,128)(2,1)} %bitcast.248, bf16[16,256,512]{2,1,0:T(8,128)(2,1)} %bitcast.247, ...), custom_call_target="tpu_custom_call" | custom-call | tf_op jit(solution)/shard_map/pallas_call | solution.py:234
  307.4 1.3 slice_add_fusion
  310.1 5.4 %fusion.34 = (bf16[4,512,512]{2,1,0:T(8,128)(2,1)}, bf16[4,512,512]{2,1,0:T(8,128)(2,1)S(1)}, bf16[4,512,512]{2,1,0:T(8,128)(2,1)}) fusion(bf16[12,512,512]{2,1,0:T(8,128)(2,1)} %get-tuple-element.23), kind=kLoop, calls=%fused_computation.163 | loop fusion | bytes 12582912 | tf_op jit(solution)/shard_map/slice | solution.py:439
  317.6 1.5 collective-permute-start.31
  319.1 3.1 constant_dynamic-slice_fusion.1
  322.8 2.3 slice.289
  325.1 1.8 copy.282
  327.5 1.7 slice.291
  329.2 1.4 copy-done.24
  330.9 1.8 copy.281
  334.1 1.7 slice.288
  336.0 1.4 copy-done.9
  338.9 2.7 collective-permute-done.33
  342.5 3.2 fusion
  346.8 1.6 fusion.9
  349.3 1.6 collective-permute-start.26
  351.8 1.4 collective-permute-start.16
  353.3 8.2 %collective-permute-done.21 = bf16[2,2,2,64,512]{4,3,2,1,0:T(8,128)(2,1)S(1)} collective-permute-done((bf16[2,2,2,64,512]{4,3,2,1,0:T(8,128)(2,1)S(1)}, bf16[2,2,2,64,512]{4,3,2,1,0:T(8,128)(2,1)S(1)}, u32[]{:S(2)}, u32[]{:S(2)}) %collective-permute-start.21) | collective-permute-done | bytes 524320 | tf_op jit(solution)/shard_map/ppermute | solution.py:286
  361.6 1.7 collective-permute-start.22
  363.3 8.0 %collective-permute-done.26 = bf16[2,2,2,64,512]{4,3,1,2,0:T(8,128)(2,1)S(1)} collective-permute-done((bf16[2,2,2,64,512]{4,3,1,2,0:T(8,128)(2,1)S(1)}, bf16[2,2,2,64,512]{4,3,1,2,0:T(8,128)(2,1)S(1)}, u32[]{:S(2)}, u32[]{:S(2)}) %collective-permute-start.26) | collective-permute-done | bytes 524320 | tf_op jit(solution)/shard_map/ppermute | solution.py:286
  372.0 11.7 %collective-permute-done.16 = bf16[2,2,2,65,512]{4,2,3,1,0:T(2,128)(2,1)S(1)} collective-permute-done((bf16[2,2,2,65,512]{4,2,3,1,0:T(2,128)(2,1)S(1)}, bf16[2,2,2,65,512]{4,2,3,1,0:T(2,128)(2,1)S(1)}, u32[]{:S(2)}, u32[]{:S(2)}) %collective-permute-start.16) | collective-permute-done | bytes 532512 | tf_op jit(solution)/shard_map/ppermute | solution.py:286
  383.9 1.6 collective-permute-start.17
  385.7 1.5 collective-permute-done.27
  387.3 1.6 collective-permute-start.28
  388.9 3.2 collective-permute-done.17
  392.2 1.8 collective-permute-start.18
  395.3 2.1 collective-permute-done.18
  397.5 1.7 collective-permute-done.24
  (231 shorter events, 45.5 us)
Async XLA Ops:
  0.6 25.8 %copy-start = (bf16[169,16]{0,1:T(8,128)(2,1)S(1)}, bf16[169,16]{0,1:T(8,128)(2,1)}, u32[]{:S(2)}) copy-start(bf16[169,16]{0,1:T(8,128)(2,1)} %param.37) | copy-start | bytes 16228
  2.8 35.3 %collective-permute-start = (bf16[64,512]{1,0:T(8,128)(2,1)}, bf16[64,512]{1,0:T(8,128)(2,1)}, u32[]{:S(2)}, u32[]{:S(2)}) collective-permute-start(bf16[64,512]{1,0:T(8,128)(2,1)} %pad_maximum_fusion.22), channel_id=1, source_target_pairs={{0,16},{1,17},{2,18},{3,19},{4,20},{5,21},{6,22},{7,23},{8,24},{9,... | collective-permute-start | bytes 196616 | tf_op jit(solution)/shard_map/ppermute | solution.py:286
  6.8 32.7 %collective-permute-start.10 = (bf16[64,512]{1,0:T(8,128)(2,1)}, bf16[64,512]{1,0:T(8,128)(2,1)}, u32[]{:S(2)}, u32[]{:S(2)}) collective-permute-start(bf16[64,512]{1,0:T(8,128)(2,1)} %param.35), channel_id=1, source_target_pairs={{0,4},{1,5},{2,6},{3,7},{4,0},{5,1},{6,2},{7,3},{8,12},{9,13},{10,... | collective-permute-start | bytes 196616 | tf_op jit(solution)/shard_map/ppermute | solution.py:286
  17.3 24.6 %collective-permute-start.5 = (bf16[65,512]{1,0:T(8,128)(2,1)S(1)}, bf16[65,512]{1,0:T(8,128)(2,1)}, u32[]{:S(2)}, u32[]{:S(2)}) collective-permute-start(bf16[65,512]{1,0:T(8,128)(2,1)S(1)} %constant_dynamic-update-slice_fusion), channel_id=1, source_target_pairs={{0,8},{1,9},{2,10},{3,11},{4,12},{5,13},{6,14},{7,15},{8,0},{9,1},... | collective-permute-start | bytes 199688 | tf_op jit(solution)/shard_map/ppermute | solution.py:286
  20.1 2.7 copy-start.25
  23.7 1.7 copy-start.33
  23.7 1.9 copy-start.32
  31.7 2.5 copy-start.2
  31.7 2.6 copy-start.11
  36.4 1.7 copy-start.30
  36.4 3.1 copy-start.29
  39.0 5.0 %collective-permute-start.1 = (bf16[2,64,512]{2,1,0:T(8,128)(2,1)S(1)}, bf16[2,64,512]{2,1,0:T(8,128)(2,1)S(1)}, u32[]{:S(2)}, u32[]{:S(2)}) collective-permute-start(bf16[2,64,512]{2,1,0:T(8,128)(2,1)S(1)} %pad_maximum_fusion.18), channel_id=1, source_target_pairs={{0,8},{1,9},{2,10},{3,11},{4,12},{5,13},{6,14},{7,15},{8,0},{9,1},... | collective-permute-start | bytes 393224 | tf_op jit(solution)/shard_map/ppermute | solution.py:286
  40.4 5.0 %collective-permute-start.11 = (bf16[2,64,512]{2,1,0:T(8,128)(2,1)S(1)}, bf16[2,64,512]{2,1,0:T(8,128)(2,1)S(1)}, u32[]{:S(2)}, u32[]{:S(2)}) collective-permute-start(bf16[2,64,512]{2,1,0:T(8,128)(2,1)S(1)} %pad_maximum_fusion.19), channel_id=1, source_target_pairs={{0,2},{1,3},{2,0},{3,1},{4,6},{5,7},{6,4},{7,5},{8,10},{9,11},{10,... | collective-permute-start | bytes 393224 | tf_op jit(solution)/shard_map/ppermute | solution.py:286
  42.9 6.9 %collective-permute-start.6 = (bf16[2,65,512]{2,1,0:T(8,128)(2,1)S(1)}, bf16[2,65,512]{2,1,0:T(8,128)(2,1)S(1)}, u32[]{:S(2)}, u32[]{:S(2)}) collective-permute-start(bf16[2,65,512]{2,1,0:T(8,128)(2,1)S(1)} %pad_maximum_fusion.17), channel_id=1, source_target_pairs={{0,4},{1,5},{2,6},{3,7},{4,0},{5,1},{6,2},{7,3},{8,12},{9,13},{10,... | collective-permute-start | bytes 399368 | tf_op jit(solution)/shard_map/ppermute | solution.py:286
  44.1 8.7 %collective-permute-start.2 = (bf16[2,2,64,512]{3,2,1,0:T(8,128)(2,1)S(1)}, bf16[2,2,64,512]{3,2,1,0:T(8,128)(2,1)S(1)}, u32[]{:S(2)}, u32[]{:S(2)}) collective-permute-start(bf16[2,2,64,512]{3,2,1,0:T(8,128)(2,1)S(1)} %pad_maximum_fusion.15), channel_id=1, source_target_pairs={{0,4},{1,5},{2,6},{3,7},{4,0},{5,1},{6,2},{7,3},{8,12},{9,13},{10,... | collective-permute-start | bytes 786440 | tf_op jit(solution)/shard_map/ppermute | solution.py:286
  45.5 12.7 %collective-permute-start.12 = (bf16[2,2,64,512]{3,2,1,0:T(8,128)(2,1)S(1)}, bf16[2,2,64,512]{3,2,1,0:T(8,128)(2,1)S(1)}, u32[]{:S(2)}, u32[]{:S(2)}) collective-permute-start(bf16[2,2,64,512]{3,2,1,0:T(8,128)(2,1)S(1)} %pad_maximum_fusion.16), channel_id=1, source_target_pairs={{0,16},{1,17},{2,18},{3,19},{4,20},{5,21},{6,22},{7,23},{8,24},{9,... | collective-permute-start | bytes 786440 | tf_op jit(solution)/shard_map/ppermute | solution.py:286
  49.8 9.9 %collective-permute-start.7 = (bf16[2,2,65,512]{3,2,0,1:T(8,128)(2,1)S(1)}, bf16[2,2,65,512]{3,2,0,1:T(8,128)(2,1)S(1)}, u32[]{:S(2)}, u32[]{:S(2)}) collective-permute-start(bf16[2,2,65,512]{3,2,0,1:T(8,128)(2,1)S(1)} %pad_maximum_fusion.14), channel_id=1, source_target_pairs={{0,2},{1,3},{2,0},{3,1},{4,6},{5,7},{6,4},{7,5},{8,10},{9,11},{10,... | collective-permute-start | bytes 798728 | tf_op jit(solution)/shard_map/ppermute | solution.py:286
  52.8 14.6 %collective-permute-start.3 = (bf16[2,2,2,64,512]{4,3,2,1,0:T(8,128)(2,1)S(1)}, bf16[2,2,2,64,512]{4,3,2,1,0:T(8,128)(2,1)S(1)}, u32[]{:S(2)}, u32[]{:S(2)}) collective-permute-start(bf16[2,2,2,64,512]{4,3,2,1,0:T(8,128)(2,1)S(1)} %pad_maximum_fusion.12), channel_id=1, source_target_pairs={{0,2},{1,3},{2,0},{3,1},{4,6},{5,7},{6,4},{7,5},{8,10},{9,11},{10,... | collective-permute-start | bytes 1572872 | tf_op jit(solution)/shard_map/ppermute | solution.py:286
  58.2 20.8 %collective-permute-start.13 = (bf16[2,2,2,64,512]{4,3,2,1,0:T(8,128)(2,1)S(1)}, bf16[2,2,2,64,512]{4,3,2,1,0:T(8,128)(2,1)S(1)}, u32[]{:S(2)}, u32[]{:S(2)}) collective-permute-start(bf16[2,2,2,64,512]{4,3,2,1,0:T(8,128)(2,1)S(1)} %pad_maximum_fusion.13), channel_id=1, source_target_pairs={{0,8},{1,9},{2,10},{3,11},{4,12},{5,13},{6,14},{7,15},{8,0},{9,1},... | collective-permute-start | bytes 1572872 | tf_op jit(solution)/shard_map/ppermute | solution.py:286
  61.8 34.0 %collective-permute-start.8 = (bf16[2,2,2,65,512]{4,2,3,1,0:T(2,128)(2,1)}, bf16[2,2,2,65,512]{4,2,3,1,0:T(2,128)(2,1)}, u32[]{:S(2)}, u32[]{:S(2)}) collective-permute-start(bf16[2,2,2,65,512]{4,2,3,1,0:T(2,128)(2,1)} %copy.246), channel_id=1, source_target_pairs={{0,16},{1,17},{2,18},{3,19},{4,20},{5,21},{6,22},{7,23},{8,24},{9,... | collective-permute-start | bytes 1597448 | tf_op jit(solution)/shard_map/ppermute | solution.py:286
  67.5 13.6 %copy-start.12 = (bf16[2,2,2,1,64,512]{5,4,3,2,1,0:T(8,128)(2,1)}, bf16[2,2,2,1,64,512]{5,4,3,2,1,0:T(8,128)(2,1)S(1)}, u32[]{:S(2)}) copy-start(bf16[2,2,2,1,64,512]{5,4,3,2,1,0:T(8,128)(2,1)S(1)} %get-tuple-element.41) | copy-start | bytes 1572868
  67.5 13.6 %copy-start.14 = (bf16[2,2,2,1,64,512]{5,4,3,2,1,0:T(8,128)(2,1)}, bf16[2,2,2,1,64,512]{5,4,3,2,1,0:T(8,128)(2,1)S(1)}, u32[]{:S(2)}) copy-start(bf16[2,2,2,1,64,512]{5,4,3,2,1,0:T(8,128)(2,1)S(1)} %get-tuple-element.42) | copy-start | bytes 1572868
  68.7 12.5 %copy-start.6 = (bf16[16,14,11,512]{3,0,2,1:T(8,128)(2,1)S(1)}, bf16[16,14,11,512]{3,0,2,1:T(8,128)(2,1)}, u32[]{:S(2)}) copy-start(bf16[16,14,11,512]{3,0,2,1:T(8,128)(2,1)} %fusion.5) | copy-start | bytes 7569412
  68.7 31.9 %collective-permute-start.4 = (bf16[2,2,2,2,64,512]{5,4,3,2,1,0:T(8,128)(2,1)}, bf16[2,2,2,2,64,512]{5,4,3,2,1,0:T(8,128)(2,1)}, u32[]{:S(2)}, u32[]{:S(2)}) collective-permute-start(bf16[2,2,2,2,64,512]{5,4,3,2,1,0:T(8,128)(2,1)} %pad_maximum_fusion.9), channel_id=1, source_target_pairs={{0,1},{1,0},{2,3},{3,2},{4,5},{5,4},{6,7},{7,6},{8,9},{9,8},{10,11... | collective-permute-start | bytes 3145736 | tf_op jit(solution)/shard_map/ppermute | solution.py:286
  79.1 2.0 copy-start.18
  81.1 22.6 %collective-permute-start.14 = (bf16[2,2,2,2,64,512]{5,4,3,2,1,0:T(8,128)(2,1)}, bf16[2,2,2,2,64,512]{5,4,3,2,1,0:T(8,128)(2,1)}, u32[]{:S(2)}, u32[]{:S(2)}) collective-permute-start(bf16[2,2,2,2,64,512]{5,4,3,2,1,0:T(8,128)(2,1)} %pad_maximum_fusion.10), channel_id=1, source_target_pairs={{0,1},{1,0},{2,3},{3,2},{4,5},{5,4},{6,7},{7,6},{8,9},{9,8},{10,11... | collective-permute-start | bytes 3145736 | tf_op jit(solution)/shard_map/ppermute | solution.py:286
  88.0 2.7 copy-start.3
  93.1 2.7 copy-start.28
  97.0 1.8 copy-start.22
  97.0 1.8 copy-start.23
  98.2 2.3 copy-start.13
  98.3 2.3 copy-start.15
  98.3 8.5 %collective-permute-start.9 = (bf16[2,2,2,2,65,512]{5,3,4,2,1,0:T(2,128)(2,1)S(1)}, bf16[2,2,2,2,65,512]{5,3,4,2,1,0:T(2,128)(2,1)S(1)}, u32[]{:S(2)}, u32[]{:S(2)}) collective-permute-start(bf16[2,2,2,2,65,512]{5,3,4,2,1,0:T(2,128)(2,1)S(1)} %copy.249), channel_id=1, source_target_pairs={{0,1},{1,0},{2,3},{3,2},{4,5},{5,4},{6,7},{7,6},{8,9},{9,8},{10,11... | collective-permute-start | bytes 3194888 | tf_op jit(solution)/shard_map/ppermute | solution.py:286
  115.6 2.9 copy-start.10
  309.8 7.7 %collective-permute-start.30 = (f32[16,169]{1,0:T(8,128)S(1)}, f32[16,169]{1,0:T(8,128)S(1)}, u32[]{:S(2)}, u32[]{:S(2)}) collective-permute-start(f32[16,169]{1,0:T(8,128)S(1)} %fusion.6), channel_id=1, source_target_pairs={{0,1},{1,0},{2,3},{3,2},{4,5},{5,4},{6,7},{7,6},{8,9},{9,8},{10,11... | collective-permute-start | bytes 32456 | tf_op jit(solution)/shard_map/ppermute | solution.py:286
  315.7 6.6 %copy-start.7 = (bf16[4,32,16,512]{3,2,0,1:T(8,128)(2,1)}, bf16[4,32,16,512]{3,2,0,1:T(8,128)(2,1)S(1)}, u32[]{:S(2)}) copy-start(bf16[4,32,16,512]{3,2,0,1:T(8,128)(2,1)S(1)} %copy.275) | copy-start | bytes 6291460
  317.2 29.6 %collective-permute-start.20 = (bf16[2,2,2,2,64,512]{5,4,3,2,1,0:T(8,128)(2,1)}, bf16[2,2,2,2,64,512]{5,4,3,2,1,0:T(8,128)(2,1)}, u32[]{:S(2)}, u32[]{:S(2)}) collective-permute-start(bf16[2,2,2,2,64,512]{5,4,3,2,1,0:T(8,128)(2,1)} %dynamic-slice_bitcast_fusion), channel_id=1, source_target_pairs={{0,1},{1,0},{2,3},{3,2},{4,5},{5,4},{6,7},{7,6},{8,9},{9,8},{10,11... | collective-permute-start | bytes 3145736 | tf_op jit(solution)/shard_map/ppermute | solution.py:286
  317.6 4.7 %collective-permute-start.31 = (f32[16,169]{1,0:T(8,128)S(1)}, f32[16,169]{1,0:T(8,128)S(1)}, u32[]{:S(2)}, u32[]{:S(2)}) collective-permute-start(f32[16,169]{1,0:T(8,128)S(1)} %add.197), channel_id=1, source_target_pairs={{0,2},{1,3},{2,0},{3,1},{4,6},{5,7},{6,4},{7,5},{8,10},{9,11},{10,... | collective-permute-start | bytes 32456 | tf_op jit(solution)/shard_map/ppermute | solution.py:286
  322.3 15.4 %collective-permute-start.32 = (f32[16,169]{1,0:T(8,128)S(1)}, f32[16,169]{1,0:T(8,128)S(1)}, u32[]{:S(2)}, u32[]{:S(2)}) collective-permute-start(f32[16,169]{1,0:T(8,128)S(1)} %add.198), channel_id=1, source_target_pairs={{0,4},{1,5},{2,6},{3,7},{4,0},{5,1},{6,2},{7,3},{8,12},{9,13},{10,... | collective-permute-start | bytes 32456 | tf_op jit(solution)/shard_map/ppermute | solution.py:286
  327.4 3.1 copy-start.24
  334.1 1.7 copy-start.21
  335.9 1.6 copy-start.9
  335.9 13.0 %collective-permute-start.25 = (bf16[2,2,2,2,64,512]{5,4,2,3,0,1:T(8,128)(2,1)S(1)}, bf16[2,2,2,2,64,512]{5,4,2,3,0,1:T(8,128)(2,1)S(1)}, u32[]{:S(2)}, u32[]{:S(2)}) collective-permute-start(bf16[2,2,2,2,64,512]{5,4,2,3,0,1:T(8,128)(2,1)S(1)} %bitcast.273), channel_id=1, source_target_pairs={{0,1},{1,0},{2,3},{3,2},{4,5},{5,4},{6,7},{7,6},{8,9},{9,8},{10,11... | collective-permute-start | bytes 3145736 | tf_op jit(solution)/shard_map/ppermute | solution.py:286
  337.4 5.0 %copy-start.26 = (bf16[16,3,14,512]{3,0,2,1:T(8,128)(2,1)S(1)}, bf16[16,3,14,512]{3,0,2,1:T(8,128)(2,1)}, u32[]{:S(2)}) copy-start(bf16[16,3,14,512]{3,0,2,1:T(8,128)(2,1)} %slice.287) | copy-start | bytes 2064388
  337.7 3.8 collective-permute-start.33
  337.8 4.7 %copy-start.4 = (bf16[16,11,14,512]{3,0,2,1:T(8,128)(2,1)S(1)}, bf16[16,11,14,512]{3,0,2,1:T(8,128)(2,1)}, u32[]{:S(2)}) copy-start(bf16[16,11,14,512]{3,0,2,1:T(8,128)(2,1)} %slice.291) | copy-start | bytes 7569412
  337.8 4.7 %copy-start.5 = (bf16[16,11,14,512]{3,0,2,1:T(8,128)(2,1)S(1)}, bf16[16,11,14,512]{3,0,2,1:T(8,128)(2,1)}, u32[]{:S(2)}) copy-start(bf16[16,11,14,512]{3,0,2,1:T(8,128)(2,1)} %slice.288) | copy-start | bytes 7569412
  338.8 12.2 %collective-permute-start.15 = (bf16[2,2,2,2,65,512]{5,3,4,2,1,0:T(2,128)(2,1)S(1)}, bf16[2,2,2,2,65,512]{5,3,4,2,1,0:T(2,128)(2,1)S(1)}, u32[]{:S(2)}, u32[]{:S(2)}) collective-permute-start(bf16[2,2,2,2,65,512]{5,3,4,2,1,0:T(2,128)(2,1)S(1)} %bitcast.272), channel_id=1, source_target_pairs={{0,1},{1,0},{2,3},{3,2},{4,5},{5,4},{6,7},{7,6},{8,9},{9,8},{10,11... | collective-permute-start | bytes 3194888 | tf_op jit(solution)/shard_map/ppermute | solution.py:286
  341.5 5.3 %copy-start.8 = (bf16[4,32,16,512]{3,2,0,1:T(8,128)(2,1)S(1)}, bf16[4,32,16,512]{3,2,0,1:T(8,128)(2,1)}, u32[]{:S(2)}) copy-start(bf16[4,32,16,512]{3,2,0,1:T(8,128)(2,1)} %copy-done.7) | copy-start | bytes 6291460
  341.5 4.6 %collective-permute-start.34 = (f32[16,169]{1,0:T(8,128)S(1)}, f32[16,169]{1,0:T(8,128)S(1)}, u32[]{:S(2)}, u32[]{:S(2)}) collective-permute-start(f32[16,169]{1,0:T(8,128)S(1)} %add.200), channel_id=1, source_target_pairs={{0,16},{1,17},{2,18},{3,19},{4,20},{5,21},{6,22},{7,23},{8,24},{9,... | collective-permute-start | bytes 32456 | tf_op jit(solution)/shard_map/ppermute | solution.py:286
  345.7 3.2 copy-start.20
  348.4 13.1 %collective-permute-start.21 = (bf16[2,2,2,64,512]{4,3,2,1,0:T(8,128)(2,1)S(1)}, bf16[2,2,2,64,512]{4,3,2,1,0:T(8,128)(2,1)S(1)}, u32[]{:S(2)}, u32[]{:S(2)}) collective-permute-start(bf16[2,2,2,64,512]{4,3,2,1,0:T(8,128)(2,1)S(1)} %dynamic-slice_bitcast_fusion.2), channel_id=1, source_target_pairs={{0,2},{1,3},{2,0},{3,1},{4,6},{5,7},{6,4},{7,5},{8,10},{9,11},{10,... | collective-permute-start | bytes 1572872 | tf_op jit(solution)/shard_map/ppermute | solution.py:286
  349.3 22.0 %collective-permute-start.26 = (bf16[2,2,2,64,512]{4,3,1,2,0:T(8,128)(2,1)S(1)}, bf16[2,2,2,64,512]{4,3,1,2,0:T(8,128)(2,1)S(1)}, u32[]{:S(2)}, u32[]{:S(2)}) collective-permute-start(bf16[2,2,2,64,512]{4,3,1,2,0:T(8,128)(2,1)S(1)} %dynamic-slice_bitcast_fusion.1), channel_id=1, source_target_pairs={{0,8},{1,9},{2,10},{3,11},{4,12},{5,13},{6,14},{7,15},{8,0},{9,1},... | collective-permute-start | bytes 1572872 | tf_op jit(solution)/shard_map/ppermute | solution.py:286
  351.8 31.8 %collective-permute-start.16 = (bf16[2,2,2,65,512]{4,2,3,1,0:T(2,128)(2,1)S(1)}, bf16[2,2,2,65,512]{4,2,3,1,0:T(2,128)(2,1)S(1)}, u32[]{:S(2)}, u32[]{:S(2)}) collective-permute-start(bf16[2,2,2,65,512]{4,2,3,1,0:T(2,128)(2,1)S(1)} %bitcast.275), channel_id=1, source_target_pairs={{0,16},{1,17},{2,18},{3,19},{4,20},{5,21},{6,22},{7,23},{8,24},{9,... | collective-permute-start | bytes 1597448 | tf_op jit(solution)/shard_map/ppermute | solution.py:286
  361.6 23.9 %collective-permute-start.22 = (bf16[2,2,64,512]{3,2,1,0:T(8,128)(2,1)S(1)}, bf16[2,2,64,512]{3,2,1,0:T(8,128)(2,1)S(1)}, u32[]{:S(2)}, u32[]{:S(2)}) collective-permute-start(bf16[2,2,64,512]{3,2,1,0:T(8,128)(2,1)S(1)} %dynamic-slice_bitcast_fusion.5), channel_id=1, source_target_pairs={{0,4},{1,5},{2,6},{3,7},{4,0},{5,1},{6,2},{7,3},{8,12},{9,13},{10,... | collective-permute-start | bytes 786440 | tf_op jit(solution)/shard_map/ppermute | solution.py:286
  371.5 15.6 %collective-permute-start.27 = (bf16[2,2,64,512]{3,2,0,1:T(8,128)(2,1)S(1)}, bf16[2,2,64,512]{3,2,0,1:T(8,128)(2,1)S(1)}, u32[]{:S(2)}, u32[]{:S(2)}) collective-permute-start(bf16[2,2,64,512]{3,2,0,1:T(8,128)(2,1)S(1)} %dynamic-slice_bitcast_fusion.4), channel_id=1, source_target_pairs={{0,16},{1,17},{2,18},{3,19},{4,20},{5,21},{6,22},{7,23},{8,24},{9,... | collective-permute-start | bytes 786440 | tf_op jit(solution)/shard_map/ppermute | solution.py:286
  383.9 8.2 %collective-permute-start.17 = (bf16[2,2,65,512]{3,2,1,0:T(8,128)(2,1)S(1)}, bf16[2,2,65,512]{3,2,1,0:T(8,128)(2,1)S(1)}, u32[]{:S(2)}, u32[]{:S(2)}) collective-permute-start(bf16[2,2,65,512]{3,2,1,0:T(8,128)(2,1)S(1)} %dynamic-slice_bitcast_fusion.3), channel_id=1, source_target_pairs={{0,2},{1,3},{2,0},{3,1},{4,6},{5,7},{6,4},{7,5},{8,10},{9,11},{10,... | collective-permute-start | bytes 798728 | tf_op jit(solution)/shard_map/ppermute | solution.py:286
  385.6 8.3 %collective-permute-start.23 = (bf16[2,64,512]{2,1,0:T(8,128)(2,1)S(1)}, bf16[2,64,512]{2,1,0:T(8,128)(2,1)S(1)}, u32[]{:S(2)}, u32[]{:S(2)}) collective-permute-start(bf16[2,64,512]{2,1,0:T(8,128)(2,1)S(1)} %dynamic-slice_bitcast_fusion.8), channel_id=1, source_target_pairs={{0,8},{1,9},{2,10},{3,11},{4,12},{5,13},{6,14},{7,15},{8,0},{9,1},... | collective-permute-start | bytes 393224 | tf_op jit(solution)/shard_map/ppermute | solution.py:286
  387.2 16.5 %copy-start.1 = (bf16[169,16]{0,1:T(8,128)(2,1)S(1)}, bf16[169,16]{0,1:T(8,128)(2,1)}, u32[]{:S(2)}) copy-start(bf16[169,16]{0,1:T(8,128)(2,1)} %param.37) | copy-start | bytes 16228
  387.3 6.8 %collective-permute-start.28 = (bf16[2,64,512]{2,1,0:T(8,128)(2,1)S(1)}, bf16[2,64,512]{2,1,0:T(8,128)(2,1)S(1)}, u32[]{:S(2)}, u32[]{:S(2)}) collective-permute-start(bf16[2,64,512]{2,1,0:T(8,128)(2,1)S(1)} %dynamic-slice_bitcast_fusion.7), channel_id=1, source_target_pairs={{0,2},{1,3},{2,0},{3,1},{4,6},{5,7},{6,4},{7,5},{8,10},{9,11},{10,... | collective-permute-start | bytes 393224 | tf_op jit(solution)/shard_map/ppermute | solution.py:286
  392.2 5.2 %collective-permute-start.18 = (bf16[2,65,512]{2,1,0:T(8,128)(2,1)S(1)}, bf16[2,65,512]{2,1,0:T(8,128)(2,1)S(1)}, u32[]{:S(2)}, u32[]{:S(2)}) collective-permute-start(bf16[2,65,512]{2,1,0:T(8,128)(2,1)S(1)} %dynamic-slice_bitcast_fusion.6), channel_id=1, source_target_pairs={{0,4},{1,5},{2,6},{3,7},{4,0},{5,1},{6,2},{7,3},{8,12},{9,13},{10,... | collective-permute-start | bytes 399368 | tf_op jit(solution)/shard_map/ppermute | solution.py:286
  394.0 5.2 %collective-permute-start.24 = (bf16[64,512]{1,0:T(8,128)(2,1)S(1)}, bf16[64,512]{1,0:T(8,128)(2,1)S(1)}, u32[]{:S(2)}, u32[]{:S(2)}) collective-permute-start(bf16[64,512]{1,0:T(8,128)(2,1)S(1)} %dynamic-slice_bitcast_fusion.11), channel_id=1, source_target_pairs={{0,16},{1,17},{2,18},{3,19},{4,20},{5,21},{6,22},{7,23},{8,24},{9,... | collective-permute-start | bytes 196616 | tf_op jit(solution)/shard_map/ppermute | solution.py:286
  394.2 5.7 %collective-permute-start.29 = (bf16[64,512]{1,0:T(8,128)(2,1)S(1)}, bf16[64,512]{1,0:T(8,128)(2,1)S(1)}, u32[]{:S(2)}, u32[]{:S(2)}) collective-permute-start(bf16[64,512]{1,0:T(8,128)(2,1)S(1)} %dynamic-slice_bitcast_fusion.10), channel_id=1, source_target_pairs={{0,4},{1,5},{2,6},{3,7},{4,0},{5,1},{6,2},{7,3},{8,12},{9,13},{10,... | collective-permute-start | bytes 196616 | tf_op jit(solution)/shard_map/ppermute | solution.py:286
  397.5 4.4 %collective-permute-start.19 = (bf16[65,512]{1,0:T(8,128)(2,1)S(1)}, bf16[65,512]{1,0:T(8,128)(2,1)S(1)}, u32[]{:S(2)}, u32[]{:S(2)}) collective-permute-start(bf16[65,512]{1,0:T(8,128)(2,1)S(1)} %dynamic-slice_bitcast_fusion.9), channel_id=1, source_target_pairs={{0,8},{1,9},{2,10},{3,11},{4,12},{5,13},{6,14},{7,15},{8,0},{9,1},... | collective-permute-start | bytes 199688 | tf_op jit(solution)/shard_map/ppermute | solution.py:286
  (5 other events, 6.1 us)

commit v2 on v1

--- a/solution.py
+++ b/solution.py
@@ -62,12 +62,16 @@
     counts,
     x_ref,
     c_ref,
-    w_ref,
+    a_ref,
+    h_ref,
+    o_ref,
     v_ref,
     bias_ref,
     act_ref,
     tg_ref,
-    gw_ref,
+    ga_ref,
+    gh_ref,
+    go_ref,
     gv_ref,
     gs_ref,
     acc,
@@ -122,9 +126,9 @@
     n1_s[...] = n1
     first = (n1 * vec(0) + vec(1)).astype(BF16)
     first_s[...] = first
-    qkv_s[:, 0:width] = (nn(first, w_ref[0]) + vec(2)).astype(BF16)
-    qkv_s[:, width : 2 * width] = nn(first, w_ref[1]).astype(BF16)
-    qkv_s[:, 2 * width : 3 * width] = (nn(first, w_ref[2]) + vec(3)).astype(BF16)
+    qkv_s[:, 0:width] = (nn(first, a_ref[0]) + vec(2)).astype(BF16)
+    qkv_s[:, width : 2 * width] = nn(first, a_ref[1]).astype(BF16)
+    qkv_s[:, 2 * width : 3 * width] = (nn(first, a_ref[2]) + vec(3)).astype(BF16)
 
     def forward_pair(pr, carry):
         at = pl.ds(pl.multiple_of(pr * 128, 128), 128)
@@ -144,7 +148,7 @@
 
     lax.fori_loop(0, rows // 128, forward_pair, 0)
 
-    after = x + nn(mixed_s[...], w_ref[3]) + vec(4)
+    after = x + nn(mixed_s[...], a_ref[3]) + vec(4)
     centred = after - row_mean(after)
     r2 = lax.rsqrt(row_mean(centred * centred) + EPS)
     n2 = centred * r2
@@ -157,17 +161,17 @@
     outcome = after + vec(7)
     e2 = None
     for j in range(4):
-        hidden = nn(second, w_ref[4 + j]) + vec(8 + j)
+        hidden = nn(second, h_ref[j]) + vec(8 + j)
         cumulative = 0.5 * (1.0 + lax.erf(hidden * (1.0 / math.sqrt(2.0))))
         density = jnp.exp(-0.5 * hidden * hidden) * (1.0 / math.sqrt(2.0 * math.pi))
         active = (hidden * cumulative).astype(BF16)
         slope = cumulative + hidden * density
-        outcome = outcome + nn(active, w_ref[8 + j])
-        gh = (nt(gob, w_ref[8 + j]) * slope).astype(BF16)
+        outcome = outcome + nn(active, o_ref[j])
+        gh = (nt(gob, o_ref[j]) * slope).astype(BF16)
         acc[8 + j] += tn(active, gob)
         acc[4 + j] += tn(second, gh)
         add_vec(8 + j, low_total(gh))
-        part = nt(gh, w_ref[4 + j])
+        part = nt(gh, h_ref[j])
         e2 = part if e2 is None else e2 + part
     act_ref[...] = jnp.where(valid, outcome, 0.0).astype(BF16).reshape(act_ref.shape)
     add_vec(5, jnp.sum(e2 * n2, axis=0, keepdims=True))
@@ -177,7 +181,7 @@
     gp = grad_after.astype(BF16)
     acc[3] += tn(mixed_s[...], gp)
     add_vec(4, low_total(gp))
-    gm_s[...] = nt(gp, w_ref[3]).astype(BF16)
+    gm_s[...] = nt(gp, a_ref[3]).astype(BF16)
 
     def backward_pair(pr, carry):
         at = pl.ds(pl.multiple_of(pr * 128, 128), 128)
@@ -207,7 +211,7 @@
     for j in range(3):
         gq = gqkv_s[:, width * j : width * (j + 1)]
         acc[j] += tn(first, gq)
-        part = nt(gq, w_ref[j])
+        part = nt(gq, a_ref[j])
         e1 = part if e1 is None else e1 + part
         if j == 0:
             add_vec(2, low_total(gq))
@@ -222,11 +226,13 @@
 
     @pl.when(step == pl.num_programs(0) - 1)
     def _():
-        for j in range(12):
-            gw_ref[j] = acc[j].astype(BF16)
-
-
-def run_block(counts, x, c, weights, vectors, bias, scale):
+        for j in range(4):
+            ga_ref[j] = acc[j].astype(BF16)
+            gh_ref[j] = acc[4 + j].astype(BF16)
+            go_ref[j] = acc[8 + j].astype(BF16)
+
+
+def run_block(counts, x, c, parts, vectors, bias, scale):
     images, per_image, width = x.shape
     rows = GROUP * per_image
     whole = functools.partial(pl.BlockSpec, pipeline_mode=pl.Buffered(1))
@@ -238,26 +244,26 @@
             pl.BlockSpec(memory_space=pltpu.SMEM),
             tile,
             tile,
-            whole(weights.shape, lambda i: (0, 0, 0)),
+            *[whole(part.shape, lambda i: (0, 0, 0)) for part in parts],
             whole(vectors.shape, lambda i: (0, 0)),
             whole(bias.shape, lambda i: (0, 0, 0, 0)),
         ],
         out_specs=[
             tile,
             tile,
-            whole(weights.shape, lambda i: (0, 0, 0)),
+            *[whole(part.shape, lambda i: (0, 0, 0)) for part in parts],
             pl.BlockSpec(vectors.shape, lambda i: (0, 0)),
             pl.BlockSpec((4, 512, 128), lambda i: (0, 0, 0)),
         ],
         out_shape=[
             jax.ShapeDtypeStruct(x.shape, BF16),
             jax.ShapeDtypeStruct(x.shape, BF16),
-            jax.ShapeDtypeStruct(weights.shape, BF16),
+            *[jax.ShapeDtypeStruct(part.shape, BF16) for part in parts],
             jax.ShapeDtypeStruct(vectors.shape, F32),
             jax.ShapeDtypeStruct((4, 512, 128), F32),
         ],
         scratch_shapes=[
-            pltpu.VMEM(weights.shape, F32),
+            pltpu.VMEM((3 * parts[0].shape[0], *parts[0].shape[1:]), F32),
             pltpu.VMEM((rows // 128, 4, 512, 128), F32),
             pltpu.VMEM((rows, 3 * width), BF16),
             pltpu.VMEM((rows, width), BF16),
@@ -269,7 +275,7 @@
         compiler_params=pltpu.CompilerParams(
             dimension_semantics=("arbitrary",), vmem_limit_bytes=60 * 1024 * 1024
         ),
-    )(counts, x, c, weights, vectors, bias)
+    )(counts, x, c, *parts, vectors, bias)
 
 
 def bit_orders(count):
@@ -277,8 +283,9 @@
     far = list(range(bits - 1, 0, -1))
     orders = []
     for turn in range(3):
-        cut = (turn * len(far)) // 3
-        orders.append(far[cut:] + far[:cut] + [0])
+        rest = far[1:]
+        cut = (turn * len(rest)) // 3
+        orders.append(far[:1] + rest[cut:] + rest[:cut] + [0])
     return orders
 
 
@@ -286,9 +293,11 @@
     return lax.ppermute(array, "dp", [(i, i ^ (1 << bit)) for i in range(count)])
 
 
-def gather_all(block, order, count, me):
+def gather_all(block, order, count, me, beside=None):
     buffer = block
     for level, bit in enumerate(order):
+        if beside is not None and level == len(order) - 1:
+            buffer, beside = lax.optimization_barrier((buffer, beside))
         other = swap(buffer, bit, count)
         high = ((me >> bit) & 1) == 1
         buffer = jnp.stack(
@@ -297,7 +306,7 @@
     bits = len(order)
     back = [order.index(b) for b in range(bits - 1, -1, -1)]
     buffer = buffer.transpose(*back, *range(bits, bits + block.ndim))
-    return buffer.reshape(count, *block.shape)
+    return buffer.reshape(count, *block.shape), beside
 
 
 def scatter_sum(blocks, order, count, me):
@@ -366,21 +375,20 @@
         [qkv_weight[:, width * j : width * (j + 1)] for j in range(3)] + [proj_weight], axis=0
     )
     pack_two = jnp.concatenate(
-        [hidden_weight[:, width * j : width * (j + 1)] for j in range(4)] + [small], axis=0
-    )
-    got_one = gather_all(pack_one, orders[0], count, me)
-    got_two = gather_all(pack_two, orders[1], count, me)
-    got_three = gather_all(output_weight, orders[2], count, me)
+        [hidden_weight[:, width * j : width * (j + 1)] for j in range(4)], axis=0
+    )
+    got_small, _ = gather_all(small, orders[0], count, me)
+    got_one, x_rows = gather_all(pack_one, orders[0], count, me, to_windows(tokens))
+    got_two, c_rows = gather_all(pack_two, orders[1], count, me, to_windows(cotangent))
+    got_three, _ = gather_all(output_weight, orders[2], count, me)
 
     def joined(got):
-        return got[:, : 4 * share].reshape(count, 4, share, width).transpose(1, 0, 2, 3).reshape(
+        return got.reshape(count, 4, share, width).transpose(1, 0, 2, 3).reshape(
             4, width, width
         )
 
-    weights = jnp.concatenate(
-        [joined(got_one), joined(got_two), got_three.reshape(4, width, width)], axis=0
-    )
-    got_small = got_two[:, 4 * share, :small_len].astype(F32)
+    parts = (joined(got_one), joined(got_two), got_three.reshape(4, width, width))
+    got_small = got_small[:, 0, :small_len].astype(F32)
     vectors = jnp.concatenate(
         [
             got_small[:, : 8 * share].reshape(count, 8, share).transpose(1, 0, 2).reshape(8, width),
@@ -414,8 +422,8 @@
         axis=-2,
     ).reshape(n_win // 2, 4, 512, 128)
 
-    act, tg, gw, gv, gs = run_block(
-        counts, to_windows(tokens), to_windows(cotangent), weights, vectors, bias, scale
+    act, tg, grad_a, grad_h, grad_o, gv, gs = run_block(
+        counts, x_rows, c_rows, parts, vectors, bias, scale
     )
 
     def cut(four):
@@ -431,12 +439,11 @@
         axis=1,
     ).astype(BF16)
     small_grad = jnp.pad(small_grad, ((0, 0), (0, width - small_len)))[:, None]
-    own_one = scatter_sum(cut(gw[0:4]), orders[0][::-1], count, me).astype(F32)
-    own_two = scatter_sum(
-        jnp.concatenate([cut(gw[4:8]), small_grad], axis=1), orders[1][::-1], count, me
-    ).astype(F32)
+    own_one = scatter_sum(cut(grad_a), orders[0][::-1], count, me).astype(F32)
+    own_two = scatter_sum(cut(grad_h), orders[1][::-1], count, me).astype(F32)
+    own_small = scatter_sum(small_grad, orders[0][::-1], count, me).astype(F32)[0]
     own_three = scatter_sum(
-        gw[8:12].reshape(count, 4 * share, width), orders[2][::-1], count, me
+        grad_o.reshape(count, 4 * share, width), orders[2][::-1], count, me
     ).astype(F32)
 
     gs = gs.reshape(heads, 128, 128)
@@ -450,8 +457,6 @@
     )
     for bit in orders[0][::-1]:
         table = table + swap(table, bit, count)
-
-    own_small = own_two[4 * share]
 
     def piece(i):
         return own_small[i * share : (i + 1) * share]

time: 410 us -> 367 us (0.90)
  local copies, waits for them, and re-layouts: 80.3 us -> 45.5 us
  waiting for transfers between devices: 68.8 us -> 44 us
  starting transfers between devices: 29.4 us -> 48.2 us
    ppermute x35 -> x45, waiting for transfers between devices: 68.8 us -> 44 us  [swap(): return lax.ppermute(array, 'dp', [(i, i ^ 1 << bit) for i in range(count)])]
    ppermute x35 -> x45, starting transfers between devices: 29.4 us -> 48.2 us  [swap(): return lax.ppermute(array, 'dp', [(i, i ^ 1 << bit) for i in range(count)])]
    unnamed x77 -> x35, local copies, waits for them, and re-layouts: 16.5 us -> 8.18 us
    reshape x2, local copies, waits for them, and re-layouts: 7.09 us -> 0.03 us  [the longest x1 0.02 us: gather_all(): return (buffer.reshape(count, *block.shape), beside)]
    concatenate x2 -> x1, other arithmetic: 5.63 us -> 0.63 us  [local(): jnp.concatenate([hidden_weight[:, width * j:width * (j + 1)] for j in ran...]
    slice x2 -> x1, local copies, waits for them, and re-layouts: 5.5 us -> 0.77 us  [local(): hidden_weight[:, width * j:width * (j + 1)]]
    another operation x28 -> x37, other arithmetic: 10.1 us -> 8.39 us  [gather_all(): jnp.stack([jnp.where(high, other, buffer), jnp.where(high, buffer, other)...]
  transfers between devices with their start and end apart: 35 -> 45, of which waited for: 18 -> 18; matrix products, arithmetic and copies ran while one was open for 22% -> 19% of each run, Pallas kernels for 0% -> 0%
where the time goes in v2:
time: 367 us; the launch traced here: 363 us
  Pallas kernels  183 us (50%)
  starting transfers between devices  48.2 us (13%)
  local copies, waits for them, and re-layouts  45.5 us (12%)
  waiting for transfers between devices  44 us (12%)
  other arithmetic  37.4 us (10%)
    pallas_call x1, Pallas kernels, run_block(): pl.pallas_call(functools.partial(block_kernel, scale=scale), grid=(images...  183 us
    ppermute x45, starting transfers between devices, swap(): return lax.ppermute(array, 'dp', [(i, i ^ 1 << bit) for i in range(count)])  48.2 us
    ppermute x45, waiting for transfers between devices, swap(): return lax.ppermute(array, 'dp', [(i, i ^ 1 << bit) for i in range(count)])  44 us
    concatenate x4, other arithmetic, to_windows(): rolled = jnp.roll(field, (-SHIFT, -SHIFT), axis=(1, 2))  9.73 us
    another operation x37, other arithmetic, gather_all(): jnp.stack([jnp.where(high, other, buffer), jnp.where(high, buffer, other)...  8.39 us
    unnamed x35, local copies, waits for them, and re-layouts  8.18 us
  transfers between devices with their start and end apart: 45, of which 18 were waited for; matrix products, arithmetic and copies ran while one was open for 19% of the time, Pallas kernels for 0%

profile of v2, /device:TPU:0, one launch (start us, length us, event | category | flops | bytes accessed | tf_op | source)
XLA Modules:
  0.0 362.7 jit_solution(14719022078619619014)
XLA Ops:
  0.7 6.1 %concatenate.65 = bf16[192]{0:T(256)(128)(2,1)S(1)} concatenate(bf16[16]{0:T(256)(128)(2,1)} %param.24, bf16[16]{0:T(256)(128)(2,1)} %param.25, bf16[16]{0:T(256)(128)(2,1)} %param.27, bf16[16]{0:T(256)(128)(2,1)} %param.28, bf16[16]{0:T(256)(128)(2,1)} %param.30, bf16[16]{0:T(256)(128)(2,1)} %param.31, bf16[16]{0:T(256)(128)(2,1)} %param.32, bf16[16]{0:T(256)(128)(2,1)} %param.36, ...), dimensions={0} | concatenate | bytes 768 | tf_op jit(solution)/shard_map/concatenate | solution.py:359
  6.8 4.1 %collective-permute-start.15 = (bf16[1,512]{1,0:T(2,128)(2,1)S(1)}, bf16[1,512]{1,0:T(2,128)(2,1)S(1)}, u32[]{:S(2)}, u32[]{:S(2)}) collective-permute-start(bf16[1,512]{1,0:T(2,128)(2,1)S(1)} %reshape.249), channel_id=1, source_target_pairs={{0,16},{1,17},{2,18},{3,19},{4,20},{5,21},{6,22},{7,23},{8,24},{9,... | collective-permute-start | bytes 3080 | tf_op jit(solution)/shard_map/ppermute | solution.py:293
  13.1 1.4 pad_maximum_fusion.21
  14.4 2.9 collective-permute-start
  18.5 2.1 slice.201
  21.1 1.3 convolution_bitcast_fusion
  22.4 1.9 add.192
  24.4 1.3 broadcast_add_fusion
  25.6 1.5 slice_bitcast_fusion.1
  27.1 1.7 fusion.4
  28.9 1.9 collective-permute-start.16
  30.8 3.3 fusion.2
  34.4 1.6 collective-permute-start.17
  36.0 1.7 fusion.5
  38.1 1.6 collective-permute-start.18
  39.7 3.1 fusion.3
  43.0 3.4 select_maximum_fusion
  47.5 1.8 copy.169
  49.4 2.7 pad.30.clone
  52.5 1.8 copy.168
  54.4 2.7 pad.29.clone
  60.1 1.6 collective-permute-start.5
  62.3 1.8 collective-permute-done.1
  64.2 1.6 collective-permute-start.2
  67.0 1.4 collective-permute-start.12
  69.0 5.2 %collective-permute-done.12 = bf16[2,2,64,512]{3,2,0,1:T(8,128)(2,1)S(1)} collective-permute-done((bf16[2,2,64,512]{3,2,0,1:T(8,128)(2,1)S(1)}, bf16[2,2,64,512]{3,2,0,1:T(8,128)(2,1)S(1)}, u32[]{:S(2)}, u32[]{:S(2)}) %collective-permute-start.12) | collective-permute-done | bytes 262176 | tf_op jit(solution)/shard_map/ppermute | solution.py:293
  77.0 1.4 collective-permute-start.7
  78.4 7.7 %collective-permute-done.13 = bf16[2,2,2,64,512]{4,3,0,1,2:T(8,128)(2,1)S(1)} collective-permute-done((bf16[2,2,2,64,512]{4,3,0,1,2:T(8,128)(2,1)S(1)}, bf16[2,2,2,64,512]{4,3,0,1,2:T(8,128)(2,1)S(1)}, u32[]{:S(2)}, u32[]{:S(2)}) %collective-permute-start.13) | collective-permute-done | bytes 524320 | tf_op jit(solution)/shard_map/ppermute | solution.py:293
  88.5 1.2 select_bitcast_fusion.9
  89.9 1.2 select_bitcast_fusion.11
  92.8 1.6 copy.130
  94.9 1.5 copy.129
  96.8 1.5 copy.127
  98.3 182.9 %shard_map.306 = (bf16[16,256,512]{2,1,0:T(8,128)(2,1)}, bf16[16,256,512]{2,1,0:T(8,128)(2,1)}, bf16[4,512,512]{2,1,0:T(8,128)(2,1)}, bf16[4,512,512]{2,1,0:T(8,...) custom-call(s32[1]{0:T(128)S(6)} %copy.192.counts, ...), custom_call_target="tpu_custom_call" | custom-call | tf_op jit(solution)/shard_map/pallas_call | solution.py:240
  282.0 2.3 slice.262
  284.3 1.8 copy.166
  287.9 2.1 slice_add_fusion
  290.1 1.2 reshape.268
  292.7 1.8 constant_dynamic-slice_fusion.1
  295.2 1.8 collective-permute-start.21
  297.2 1.8 collective-permute-done.21
  299.0 1.8 collective-permute-start.22
  300.8 1.8 fusion
  302.9 1.4 collective-permute-start.23
  305.2 1.8 copy.165
  308.0 1.5 collective-permute-start.41
  309.5 2.7 collective-permute-start.24
  312.2 2.0 fusion.1
  315.4 2.6 collective-permute-done.42
  318.0 1.3 collective-permute-start.43
  319.9 1.8 collective-permute-done.43
  322.6 3.8 %collective-permute-done.44 = f32[16,169]{1,0:T(8,128)S(1)} collective-permute-done((f32[16,169]{1,0:T(8,128)S(1)}, f32[16,169]{1,0:T(8,128)S(1)}, u32[]{:S(2)}, u32[]{:S(2)}) %collective-permute-start.44) | collective-permute-done | bytes 10848 | tf_op jit(solution)/shard_map/ppermute | solution.py:293
  330.9 7.2 %collective-permute-done.36 = bf16[2,2,2,64,512]{4,3,0,2,1:T(8,128)(2,1)S(1)} collective-permute-done((bf16[2,2,2,64,512]{4,3,0,2,1:T(8,128)(2,1)S(1)}, bf16[2,2,2,64,512]{4,3,0,2,1:T(8,128)(2,1)S(1)}, u32[]{:S(2)}, u32[]{:S(2)}) %collective-permute-start.36) | collective-permute-done | bytes 524320 | tf_op jit(solution)/shard_map/ppermute | solution.py:293
  338.3 1.9 collective-permute-start.37
  340.8 1.9 collective-permute-done.31
  342.8 1.5 collective-permute-start.32
  344.4 1.3 collective-permute-done.37
  345.8 1.5 collective-permute-start.38
  348.0 1.2 collective-permute-done.32
  351.8 1.2 collective-permute-done.28
  353.1 1.4 collective-permute-start.29
  354.5 1.7 collective-permute-start.34
  356.2 2.1 collective-permute-done.29
  359.0 1.5 collective-permute-done.34
  (227 shorter events, 39.9 us)
Async XLA Ops:
  0.6 20.5 %copy-start = (bf16[169,16]{0,1:T(8,128)(2,1)S(1)}, bf16[169,16]{0,1:T(8,128)(2,1)}, u32[]{:S(2)}) copy-start(bf16[169,16]{0,1:T(8,128)(2,1)} %param.37) | copy-start | bytes 16228
  6.8 22.0 %collective-permute-start.15 = (bf16[1,512]{1,0:T(2,128)(2,1)S(1)}, bf16[1,512]{1,0:T(2,128)(2,1)S(1)}, u32[]{:S(2)}, u32[]{:S(2)}) collective-permute-start(bf16[1,512]{1,0:T(2,128)(2,1)S(1)} %reshape.249), channel_id=1, source_target_pairs={{0,16},{1,17},{2,18},{3,19},{4,20},{5,21},{6,22},{7,23},{8,24},{9,... | collective-permute-start | bytes 3080 | tf_op jit(solution)/shard_map/ppermute | solution.py:293
  12.3 46.8 %collective-permute-start.4 = (bf16[64,512]{1,0:T(8,128)(2,1)}, bf16[64,512]{1,0:T(8,128)(2,1)}, u32[]{:S(2)}, u32[]{:S(2)}) collective-permute-start(bf16[64,512]{1,0:T(8,128)(2,1)} %pad_maximum_fusion.22), channel_id=1, source_target_pairs={{0,16},{1,17},{2,18},{3,19},{4,20},{5,21},{6,22},{7,23},{8,24},{9,... | collective-permute-start | bytes 196616 | tf_op jit(solution)/shard_map/ppermute | solution.py:293
  14.4 43.0 %collective-permute-start = (bf16[64,512]{1,0:T(8,128)(2,1)}, bf16[64,512]{1,0:T(8,128)(2,1)}, u32[]{:S(2)}, u32[]{:S(2)}) collective-permute-start(bf16[64,512]{1,0:T(8,128)(2,1)} %pad_maximum_fusion.21), channel_id=1, source_target_pairs={{0,16},{1,17},{2,18},{3,19},{4,20},{5,21},{6,22},{7,23},{8,24},{9,... | collective-permute-start | bytes 196616 | tf_op jit(solution)/shard_map/ppermute | solution.py:293
  17.3 41.8 %collective-permute-start.10 = (bf16[64,512]{1,0:T(8,128)(2,1)}, bf16[64,512]{1,0:T(8,128)(2,1)}, u32[]{:S(2)}, u32[]{:S(2)}) collective-permute-start(bf16[64,512]{1,0:T(8,128)(2,1)} %param.35), channel_id=1, source_target_pairs={{0,16},{1,17},{2,18},{3,19},{4,20},{5,21},{6,22},{7,23},{8,24},{9,... | collective-permute-start | bytes 196616 | tf_op jit(solution)/shard_map/ppermute | solution.py:293
  18.5 2.1 copy-start.12
  18.5 2.3 copy-start.11
  28.8 5.2 %copy-start.5 = (bf16[16,14,14,512]{3,0,2,1:T(8,128)(2,1)S(1)}, bf16[16,14,14,512]{3,0,2,1:T(8,128)(2,1)}, u32[]{:S(2)}) copy-start(bf16[16,14,14,512]{3,0,2,1:T(8,128)(2,1)} %param.19) | copy-start | bytes 9633796
  28.9 5.5 %collective-permute-start.16 = (bf16[2,1,512]{2,0,1:T(2,128)(2,1)S(1)}, bf16[2,1,512]{2,0,1:T(2,128)(2,1)S(1)}, u32[]{:S(2)}, u32[]{:S(2)}) collective-permute-start(bf16[2,1,512]{2,0,1:T(2,128)(2,1)S(1)} %pad_maximum_fusion.27), channel_id=1, source_target_pairs={{0,8},{1,9},{2,10},{3,11},{4,12},{5,13},{6,14},{7,15},{8,0},{9,1},... | collective-permute-start | bytes 6152 | tf_op jit(solution)/shard_map/ppermute | solution.py:293
  34.4 3.7 %collective-permute-start.17 = (bf16[2,2,1,512]{3,0,2,1:T(2,128)(2,1)S(1)}, bf16[2,2,1,512]{3,0,2,1:T(2,128)(2,1)S(1)}, u32[]{:S(2)}, u32[]{:S(2)}) collective-permute-start(bf16[2,2,1,512]{3,0,2,1:T(2,128)(2,1)S(1)} %pad_maximum_fusion.26), channel_id=1, source_target_pairs={{0,4},{1,5},{2,6},{3,7},{4,0},{5,1},{6,2},{7,3},{8,12},{9,13},{10,... | collective-permute-start | bytes 12296 | tf_op jit(solution)/shard_map/ppermute | solution.py:293
  38.1 4.7 %collective-permute-start.18 = (bf16[2,2,2,1,512]{4,0,1,3,2:T(2,128)(2,1)S(1)}, bf16[2,2,2,1,512]{4,0,1,3,2:T(2,128)(2,1)S(1)}, u32[]{:S(2)}, u32[]{:S(2)}) collective-permute-start(bf16[2,2,2,1,512]{4,0,1,3,2:T(2,128)(2,1)S(1)} %pad_maximum_fusion.25), channel_id=1, source_target_pairs={{0,2},{1,3},{2,0},{3,1},{4,6},{5,7},{6,4},{7,5},{8,10},{9,11},{10,... | collective-permute-start | bytes 24584 | tf_op jit(solution)/shard_map/ppermute | solution.py:293
  42.8 4.3 %copy-start.2 = (bf16[16,14,14,512]{3,0,2,1:T(8,128)(2,1)S(1)}, bf16[16,14,14,512]{3,0,2,1:T(8,128)(2,1)}, u32[]{:S(2)}) copy-start(bf16[16,14,14,512]{3,0,2,1:T(8,128)(2,1)} %fusion.2) | copy-start | bytes 9633796
  42.9 14.3 %collective-permute-start.19 = (bf16[2,2,2,2,1,512]{5,0,1,2,4,3:T(2,128)(2,1)S(1)}, bf16[2,2,2,2,1,512]{5,0,1,2,4,3:T(2,128)(2,1)S(1)}, u32[]{:S(2)}, u32[]{:S(2)}) collective-permute-start(bf16[2,2,2,2,1,512]{5,0,1,2,4,3:T(2,128)(2,1)S(1)} %pad_maximum_fusion.24), channel_id=1, source_target_pairs={{0,1},{1,0},{2,3},{3,2},{4,5},{5,4},{6,7},{7,6},{8,9},{9,8},{10,11... | collective-permute-start | bytes 49160 | tf_op jit(solution)/shard_map/ppermute | solution.py:293
  49.4 2.7 copy-start.3
  54.4 3.0 copy-start.9
  54.4 4.7 %copy-start.8 = (bf16[64,512]{1,0:T(8,128)(2,1)S(1)}, bf16[64,512]{1,0:T(8,128)(2,1)}, u32[]{:S(2)}) copy-start(bf16[64,512]{1,0:T(8,128)(2,1)} %param.35) | copy-start | bytes 196612
  58.3 5.8 %collective-permute-start.1 = (bf16[2,64,512]{2,1,0:T(8,128)(2,1)S(1)}, bf16[2,64,512]{2,1,0:T(8,128)(2,1)S(1)}, u32[]{:S(2)}, u32[]{:S(2)}) collective-permute-start(bf16[2,64,512]{2,1,0:T(8,128)(2,1)S(1)} %pad_maximum_fusion.16), channel_id=1, source_target_pairs={{0,8},{1,9},{2,10},{3,11},{4,12},{5,13},{6,14},{7,15},{8,0},{9,1},... | collective-permute-start | bytes 393224 | tf_op jit(solution)/shard_map/ppermute | solution.py:293
  60.1 8.3 %collective-permute-start.5 = (bf16[2,64,512]{2,1,0:T(8,128)(2,1)S(1)}, bf16[2,64,512]{2,1,0:T(8,128)(2,1)S(1)}, u32[]{:S(2)}, u32[]{:S(2)}) collective-permute-start(bf16[2,64,512]{2,1,0:T(8,128)(2,1)S(1)} %pad_maximum_fusion.17), channel_id=1, source_target_pairs={{0,4},{1,5},{2,6},{3,7},{4,0},{5,1},{6,2},{7,3},{8,12},{9,13},{10,... | collective-permute-start | bytes 393224 | tf_op jit(solution)/shard_map/ppermute | solution.py:293
  61.7 5.2 %collective-permute-start.11 = (bf16[2,64,512]{2,1,0:T(8,128)(2,1)S(1)}, bf16[2,64,512]{2,1,0:T(8,128)(2,1)S(1)}, u32[]{:S(2)}, u32[]{:S(2)}) collective-permute-start(bf16[2,64,512]{2,1,0:T(8,128)(2,1)S(1)} %pad_maximum_fusion.18), channel_id=1, source_target_pairs={{0,2},{1,3},{2,0},{3,1},{4,6},{5,7},{6,4},{7,5},{8,10},{9,11},{10,... | collective-permute-start | bytes 393224 | tf_op jit(solution)/shard_map/ppermute | solution.py:293
  64.2 10.7 %collective-permute-start.2 = (bf16[2,2,64,512]{3,2,1,0:T(8,128)(2,1)S(1)}, bf16[2,2,64,512]{3,2,1,0:T(8,128)(2,1)S(1)}, u32[]{:S(2)}, u32[]{:S(2)}) collective-permute-start(bf16[2,2,64,512]{3,2,1,0:T(8,128)(2,1)S(1)} %pad_maximum_fusion.13), channel_id=1, source_target_pairs={{0,4},{1,5},{2,6},{3,7},{4,0},{5,1},{6,2},{7,3},{8,12},{9,13},{10,... | collective-permute-start | bytes 786440 | tf_op jit(solution)/shard_map/ppermute | solution.py:293
  67.0 7.2 %collective-permute-start.12 = (bf16[2,2,64,512]{3,2,0,1:T(8,128)(2,1)S(1)}, bf16[2,2,64,512]{3,2,0,1:T(8,128)(2,1)S(1)}, u32[]{:S(2)}, u32[]{:S(2)}) collective-permute-start(bf16[2,2,64,512]{3,2,0,1:T(8,128)(2,1)S(1)} %pad_maximum_fusion.15), channel_id=1, source_target_pairs={{0,8},{1,9},{2,10},{3,11},{4,12},{5,13},{6,14},{7,15},{8,0},{9,1},... | collective-permute-start | bytes 786440 | tf_op jit(solution)/shard_map/ppermute | solution.py:293
  68.4 7.7 %collective-permute-start.6 = (bf16[2,2,64,512]{3,2,0,1:T(8,128)(2,1)S(1)}, bf16[2,2,64,512]{3,2,0,1:T(8,128)(2,1)S(1)}, u32[]{:S(2)}, u32[]{:S(2)}) collective-permute-start(bf16[2,2,64,512]{3,2,0,1:T(8,128)(2,1)S(1)} %pad_maximum_fusion.14), channel_id=1, source_target_pairs={{0,2},{1,3},{2,0},{3,1},{4,6},{5,7},{6,4},{7,5},{8,10},{9,11},{10,... | collective-permute-start | bytes 786440 | tf_op jit(solution)/shard_map/ppermute | solution.py:293
  74.2 11.9 %collective-permute-start.13 = (bf16[2,2,2,64,512]{4,3,0,1,2:T(8,128)(2,1)S(1)}, bf16[2,2,2,64,512]{4,3,0,1,2:T(8,128)(2,1)S(1)}, u32[]{:S(2)}, u32[]{:S(2)}) collective-permute-start(bf16[2,2,2,64,512]{4,3,0,1,2:T(8,128)(2,1)S(1)} %pad_maximum_fusion.12), channel_id=1, source_target_pairs={{0,4},{1,5},{2,6},{3,7},{4,0},{5,1},{6,2},{7,3},{8,12},{9,13},{10,... | collective-permute-start | bytes 1572872 | tf_op jit(solution)/shard_map/ppermute | solution.py:293
  75.7 14.2 %collective-permute-start.3 = (bf16[2,2,2,64,512]{4,3,2,1,0:T(8,128)(2,1)}, bf16[2,2,2,64,512]{4,3,2,1,0:T(8,128)(2,1)}, u32[]{:S(2)}, u32[]{:S(2)}) collective-permute-start(bf16[2,2,2,64,512]{4,3,2,1,0:T(8,128)(2,1)} %pad_maximum_fusion.10), channel_id=1, source_target_pairs={{0,2},{1,3},{2,0},{3,1},{4,6},{5,7},{6,4},{7,5},{8,10},{9,11},{10,... | collective-permute-start | bytes 1572872 | tf_op jit(solution)/shard_map/ppermute | solution.py:293
  77.0 11.5 %collective-permute-start.7 = (bf16[2,2,2,64,512]{4,3,0,1,2:T(8,128)(2,1)}, bf16[2,2,2,64,512]{4,3,0,1,2:T(8,128)(2,1)}, u32[]{:S(2)}, u32[]{:S(2)}) collective-permute-start(bf16[2,2,2,64,512]{4,3,0,1,2:T(8,128)(2,1)} %pad_maximum_fusion.11), channel_id=1, source_target_pairs={{0,8},{1,9},{2,10},{3,11},{4,12},{5,13},{6,14},{7,15},{8,0},{9,1},... | collective-permute-start | bytes 1572872 | tf_op jit(solution)/shard_map/ppermute | solution.py:293
  87.3 5.2 %collective-permute-start.14 = (bf16[2,2,2,2,64,512]{5,4,0,1,2,3:T(8,128)(2,1)}, bf16[2,2,2,2,64,512]{5,4,0,1,2,3:T(8,128)(2,1)S(1)}, u32[]{:S(2)}, u32[]{:S(2)}) collective-permute-start(bf16[2,2,2,2,64,512]{5,4,0,1,2,3:T(8,128)(2,1)} %pad_maximum_fusion.9), channel_id=1, source_target_pairs={{0,1},{1,0},{2,3},{3,2},{4,5},{5,4},{6,7},{7,6},{8,9},{9,8},{10,11... | collective-permute-start | bytes 3145736 | tf_op jit(solution)/shard_map/ppermute | solution.py:293
  89.8 4.6 %collective-permute-start.9 = (bf16[2,2,2,2,64,512]{5,4,0,1,2,3:T(8,128)(2,1)S(1)}, bf16[2,2,2,2,64,512]{5,4,0,1,2,3:T(8,128)(2,1)S(1)}, u32[]{:S(2)}, u32[]{:S(2)}) collective-permute-start(bf16[2,2,2,2,64,512]{5,4,0,1,2,3:T(8,128)(2,1)S(1)} %pad_maximum_fusion.8), channel_id=1, source_target_pairs={{0,1},{1,0},{2,3},{3,2},{4,5},{5,4},{6,7},{7,6},{8,9},{9,8},{10,11... | collective-permute-start | bytes 3145736 | tf_op jit(solution)/shard_map/ppermute | solution.py:293
  91.2 5.3 %collective-permute-start.8 = (bf16[2,2,2,2,64,512]{5,4,3,2,1,0:T(8,128)(2,1)S(1)}, bf16[2,2,2,2,64,512]{5,4,3,2,1,0:T(8,128)(2,1)S(1)}, u32[]{:S(2)}, u32[]{:S(2)}) collective-permute-start(bf16[2,2,2,2,64,512]{5,4,3,2,1,0:T(8,128)(2,1)S(1)} %pad_maximum_fusion.7), channel_id=1, source_target_pairs={{0,1},{1,0},{2,3},{3,2},{4,5},{5,4},{6,7},{7,6},{8,9},{9,8},{10,11... | collective-permute-start | bytes 3145736 | tf_op jit(solution)/shard_map/ppermute | solution.py:293
  282.0 2.3 copy-start.10
  286.6 0.7 slice-start
  286.6 0.8 slice-start.1
  287.9 7.3 %collective-permute-start.20 = (bf16[2,2,2,2,1,512]{5,3,2,1,0,4:T(2,128)(2,1)S(1)}, bf16[2,2,2,2,1,512]{5,3,2,1,0,4:T(2,128)(2,1)S(1)}, u32[]{:S(2)}, u32[]{:S(2)}) collective-permute-start(bf16[2,2,2,2,1,512]{5,3,2,1,0,4:T(2,128)(2,1)S(1)} %bitcast.331), channel_id=1, source_target_pairs={{0,1},{1,0},{2,3},{3,2},{4,5},{5,4},{6,7},{7,6},{8,9},{9,8},{10,11... | collective-permute-start | bytes 49160 | tf_op jit(solution)/shard_map/ppermute | solution.py:293
  292.2 15.8 %collective-permute-start.40 = (f32[16,169]{1,0:T(8,128)S(1)}, f32[16,169]{1,0:T(8,128)S(1)}, u32[]{:S(2)}, u32[]{:S(2)}) collective-permute-start(f32[16,169]{1,0:T(8,128)S(1)} %fusion.6), channel_id=1, source_target_pairs={{0,1},{1,0},{2,3},{3,2},{4,5},{5,4},{6,7},{7,6},{8,9},{9,8},{10,11... | collective-permute-start | bytes 32456 | tf_op jit(solution)/shard_map/ppermute | solution.py:293
  292.7 2.2 copy-start.7
  294.6 32.4 %collective-permute-start.35 = (bf16[2,2,2,2,64,512]{5,4,0,3,1,2:T(8,128)(2,1)S(1)}, bf16[2,2,2,2,64,512]{5,4,0,3,1,2:T(8,128)(2,1)S(1)}, u32[]{:S(2)}, u32[]{:S(2)}) collective-permute-start(bf16[2,2,2,2,64,512]{5,4,0,3,1,2:T(8,128)(2,1)S(1)} %bitcast.323), channel_id=1, source_target_pairs={{0,1},{1,0},{2,3},{3,2},{4,5},{5,4},{6,7},{7,6},{8,9},{9,8},{10,11... | collective-permute-start | bytes 3145736 | tf_op jit(solution)/shard_map/ppermute | solution.py:293
  295.2 3.7 %collective-permute-start.21 = (bf16[2,2,2,1,512]{4,2,1,0,3:T(2,128)(2,1)S(1)}, bf16[2,2,2,1,512]{4,2,1,0,3:T(2,128)(2,1)S(1)}, u32[]{:S(2)}, u32[]{:S(2)}) collective-permute-start(bf16[2,2,2,1,512]{4,2,1,0,3:T(2,128)(2,1)S(1)} %bitcast.332), channel_id=1, source_target_pairs={{0,2},{1,3},{2,0},{3,1},{4,6},{5,7},{6,4},{7,5},{8,10},{9,11},{10,... | collective-permute-start | bytes 24584 | tf_op jit(solution)/shard_map/ppermute | solution.py:293
  297.1 32.5 %collective-permute-start.30 = (bf16[2,2,2,2,64,512]{5,4,3,2,1,0:T(8,128)(2,1)S(1)}, bf16[2,2,2,2,64,512]{5,4,3,2,1,0:T(8,128)(2,1)S(1)}, u32[]{:S(2)}, u32[]{:S(2)}) collective-permute-start(bf16[2,2,2,2,64,512]{5,4,3,2,1,0:T(8,128)(2,1)S(1)} %dynamic-slice_bitcast_fusion), channel_id=1, source_target_pairs={{0,1},{1,0},{2,3},{3,2},{4,5},{5,4},{6,7},{7,6},{8,9},{9,8},{10,11... | collective-permute-start | bytes 3145736 | tf_op jit(solution)/shard_map/ppermute | solution.py:293
  299.0 3.6 %copy-start.6 = (bf16[4,512,512]{2,1,0:T(8,128)(2,1)S(1)}, bf16[4,512,512]{2,1,0:T(8,128)(2,1)}, u32[]{:S(2)}) copy-start(bf16[4,512,512]{2,1,0:T(8,128)(2,1)} %get-tuple-element.34) | copy-start | bytes 6291460
  299.0 3.8 %collective-permute-start.22 = (bf16[2,2,1,512]{3,1,0,2:T(2,128)(2,1)S(1)}, bf16[2,2,1,512]{3,1,0,2:T(2,128)(2,1)S(1)}, u32[]{:S(2)}, u32[]{:S(2)}) collective-permute-start(bf16[2,2,1,512]{3,1,0,2:T(2,128)(2,1)S(1)} %bitcast.333), channel_id=1, source_target_pairs={{0,4},{1,5},{2,6},{3,7},{4,0},{5,1},{6,2},{7,3},{8,12},{9,13},{10,... | collective-permute-start | bytes 12296 | tf_op jit(solution)/shard_map/ppermute | solution.py:293
  302.7 2.2 copy-start.4
  302.9 6.6 %collective-permute-start.23 = (bf16[2,1,512]{2,0,1:T(2,128)(2,1)S(1)}, bf16[2,1,512]{2,0,1:T(2,128)(2,1)S(1)}, u32[]{:S(2)}, u32[]{:S(2)}) collective-permute-start(bf16[2,1,512]{2,0,1:T(2,128)(2,1)S(1)} %bitcast.334), channel_id=1, source_target_pairs={{0,8},{1,9},{2,10},{3,11},{4,12},{5,13},{6,14},{7,15},{8,0},{9,1},... | collective-permute-start | bytes 6152 | tf_op jit(solution)/shard_map/ppermute | solution.py:293
  307.9 20.7 %collective-permute-start.25 = (bf16[2,2,2,2,64,512]{5,4,3,2,1,0:T(8,128)(2,1)S(1)}, bf16[2,2,2,2,64,512]{5,4,3,2,1,0:T(8,128)(2,1)S(1)}, u32[]{:S(2)}, u32[]{:S(2)}) collective-permute-start(bf16[2,2,2,2,64,512]{5,4,3,2,1,0:T(8,128)(2,1)S(1)} %dynamic-slice_bitcast_fusion.1), channel_id=1, source_target_pairs={{0,1},{1,0},{2,3},{3,2},{4,5},{5,4},{6,7},{7,6},{8,9},{9,8},{10,11... | collective-permute-start | bytes 3145736 | tf_op jit(solution)/shard_map/ppermute | solution.py:293
  308.0 6.2 %collective-permute-start.41 = (f32[16,169]{1,0:T(8,128)S(1)}, f32[16,169]{1,0:T(8,128)S(1)}, u32[]{:S(2)}, u32[]{:S(2)}) collective-permute-start(f32[16,169]{1,0:T(8,128)S(1)} %add.228), channel_id=1, source_target_pairs={{0,2},{1,3},{2,0},{3,1},{4,6},{5,7},{6,4},{7,5},{8,10},{9,11},{10,... | collective-permute-start | bytes 32456 | tf_op jit(solution)/shard_map/ppermute | solution.py:293
  309.5 5.8 %collective-permute-start.24 = (bf16[1,512]{1,0:T(2,128)(2,1)S(1)}, bf16[1,512]{1,0:T(2,128)(2,1)S(1)}, u32[]{:S(2)}, u32[]{:S(2)}) collective-permute-start(bf16[1,512]{1,0:T(2,128)(2,1)S(1)} %fusion.52), channel_id=1, source_target_pairs={{0,16},{1,17},{2,18},{3,19},{4,20},{5,21},{6,22},{7,23},{8,24},{9,... | collective-permute-start | bytes 3080 | tf_op jit(solution)/shard_map/ppermute | solution.py:293
  314.2 3.8 %collective-permute-start.42 = (f32[16,169]{1,0:T(8,128)S(1)}, f32[16,169]{1,0:T(8,128)S(1)}, u32[]{:S(2)}, u32[]{:S(2)}) collective-permute-start(f32[16,169]{1,0:T(8,128)S(1)} %add.229), channel_id=1, source_target_pairs={{0,4},{1,5},{2,6},{3,7},{4,0},{5,1},{6,2},{7,3},{8,12},{9,13},{10,... | collective-permute-start | bytes 32456 | tf_op jit(solution)/shard_map/ppermute | solution.py:293
  318.0 3.7 %collective-permute-start.43 = (f32[16,169]{1,0:T(8,128)S(1)}, f32[16,169]{1,0:T(8,128)S(1)}, u32[]{:S(2)}, u32[]{:S(2)}) collective-permute-start(f32[16,169]{1,0:T(8,128)S(1)} %add.230), channel_id=1, source_target_pairs={{0,8},{1,9},{2,10},{3,11},{4,12},{5,13},{6,14},{7,15},{8,0},{9,1},... | collective-permute-start | bytes 32456 | tf_op jit(solution)/shard_map/ppermute | solution.py:293
  321.8 4.6 %collective-permute-start.44 = (f32[16,169]{1,0:T(8,128)S(1)}, f32[16,169]{1,0:T(8,128)S(1)}, u32[]{:S(2)}, u32[]{:S(2)}) collective-permute-start(f32[16,169]{1,0:T(8,128)S(1)} %add.231), channel_id=1, source_target_pairs={{0,16},{1,17},{2,18},{3,19},{4,20},{5,21},{6,22},{7,23},{8,24},{9,... | collective-permute-start | bytes 32456 | tf_op jit(solution)/shard_map/ppermute | solution.py:293
  327.5 10.6 %collective-permute-start.36 = (bf16[2,2,2,64,512]{4,3,0,2,1:T(8,128)(2,1)S(1)}, bf16[2,2,2,64,512]{4,3,0,2,1:T(8,128)(2,1)S(1)}, u32[]{:S(2)}, u32[]{:S(2)}) collective-permute-start(bf16[2,2,2,64,512]{4,3,0,2,1:T(8,128)(2,1)S(1)} %dynamic-slice_bitcast_fusion.2), channel_id=1, source_target_pairs={{0,4},{1,5},{2,6},{3,7},{4,0},{5,1},{6,2},{7,3},{8,12},{9,13},{10,... | collective-permute-start | bytes 1572872 | tf_op jit(solution)/shard_map/ppermute | solution.py:293
  329.0 11.2 %collective-permute-start.26 = (bf16[2,2,2,64,512]{4,3,2,1,0:T(8,128)(2,1)S(1)}, bf16[2,2,2,64,512]{4,3,2,1,0:T(8,128)(2,1)S(1)}, u32[]{:S(2)}, u32[]{:S(2)}) collective-permute-start(bf16[2,2,2,64,512]{4,3,2,1,0:T(8,128)(2,1)S(1)} %dynamic-slice_bitcast_fusion.4), channel_id=1, source_target_pairs={{0,2},{1,3},{2,0},{3,1},{4,6},{5,7},{6,4},{7,5},{8,10},{9,11},{10,... | collective-permute-start | bytes 1572872 | tf_op jit(solution)/shard_map/ppermute | solution.py:293
  330.0 12.6 %collective-permute-start.31 = (bf16[2,2,2,64,512]{4,3,2,1,0:T(8,128)(2,1)S(1)}, bf16[2,2,2,64,512]{4,3,2,1,0:T(8,128)(2,1)S(1)}, u32[]{:S(2)}, u32[]{:S(2)}) collective-permute-start(bf16[2,2,2,64,512]{4,3,2,1,0:T(8,128)(2,1)S(1)} %dynamic-slice_bitcast_fusion.3), channel_id=1, source_target_pairs={{0,8},{1,9},{2,10},{3,11},{4,12},{5,13},{6,14},{7,15},{8,0},{9,1},... | collective-permute-start | bytes 1572872 | tf_op jit(solution)/shard_map/ppermute | solution.py:293
  338.3 7.4 %collective-permute-start.37 = (bf16[2,2,64,512]{3,2,0,1:T(8,128)(2,1)S(1)}, bf16[2,2,64,512]{3,2,0,1:T(8,128)(2,1)S(1)}, u32[]{:S(2)}, u32[]{:S(2)}) collective-permute-start(bf16[2,2,64,512]{3,2,0,1:T(8,128)(2,1)S(1)} %dynamic-slice_bitcast_fusion.5), channel_id=1, source_target_pairs={{0,8},{1,9},{2,10},{3,11},{4,12},{5,13},{6,14},{7,15},{8,0},{9,1},... | collective-permute-start | bytes 786440 | tf_op jit(solution)/shard_map/ppermute | solution.py:293
  340.4 6.9 %collective-permute-start.27 = (bf16[2,2,64,512]{3,2,1,0:T(8,128)(2,1)S(1)}, bf16[2,2,64,512]{3,2,1,0:T(8,128)(2,1)S(1)}, u32[]{:S(2)}, u32[]{:S(2)}) collective-permute-start(bf16[2,2,64,512]{3,2,1,0:T(8,128)(2,1)S(1)} %dynamic-slice_bitcast_fusion.7), channel_id=1, source_target_pairs={{0,4},{1,5},{2,6},{3,7},{4,0},{5,1},{6,2},{7,3},{8,12},{9,13},{10,... | collective-permute-start | bytes 786440 | tf_op jit(solution)/shard_map/ppermute | solution.py:293
  342.8 6.4 %collective-permute-start.32 = (bf16[2,2,64,512]{3,2,1,0:T(8,128)(2,1)S(1)}, bf16[2,2,64,512]{3,2,1,0:T(8,128)(2,1)S(1)}, u32[]{:S(2)}, u32[]{:S(2)}) collective-permute-start(bf16[2,2,64,512]{3,2,1,0:T(8,128)(2,1)S(1)} %dynamic-slice_bitcast_fusion.6), channel_id=1, source_target_pairs={{0,2},{1,3},{2,0},{3,1},{4,6},{5,7},{6,4},{7,5},{8,10},{9,11},{10,... | collective-permute-start | bytes 786440 | tf_op jit(solution)/shard_map/ppermute | solution.py:293
  345.8 5.0 %collective-permute-start.38 = (bf16[2,64,512]{2,1,0:T(8,128)(2,1)S(1)}, bf16[2,64,512]{2,1,0:T(8,128)(2,1)S(1)}, u32[]{:S(2)}, u32[]{:S(2)}) collective-permute-start(bf16[2,64,512]{2,1,0:T(8,128)(2,1)S(1)} %dynamic-slice_bitcast_fusion.8), channel_id=1, source_target_pairs={{0,2},{1,3},{2,0},{3,1},{4,6},{5,7},{6,4},{7,5},{8,10},{9,11},{10,... | collective-permute-start | bytes 393224 | tf_op jit(solution)/shard_map/ppermute | solution.py:293
  347.3 15.2 %copy-start.1 = (bf16[169,16]{0,1:T(8,128)(2,1)S(1)}, bf16[169,16]{0,1:T(8,128)(2,1)}, u32[]{:S(2)}) copy-start(bf16[169,16]{0,1:T(8,128)(2,1)} %param.37) | copy-start | bytes 16228
  347.4 5.6 %collective-permute-start.28 = (bf16[2,64,512]{2,1,0:T(8,128)(2,1)S(1)}, bf16[2,64,512]{2,1,0:T(8,128)(2,1)S(1)}, u32[]{:S(2)}, u32[]{:S(2)}) collective-permute-start(bf16[2,64,512]{2,1,0:T(8,128)(2,1)S(1)} %dynamic-slice_bitcast_fusion.10), channel_id=1, source_target_pairs={{0,8},{1,9},{2,10},{3,11},{4,12},{5,13},{6,14},{7,15},{8,0},{9,1},... | collective-permute-start | bytes 393224 | tf_op jit(solution)/shard_map/ppermute | solution.py:293
  349.4 5.1 %collective-permute-start.33 = (bf16[2,64,512]{2,1,0:T(8,128)(2,1)S(1)}, bf16[2,64,512]{2,1,0:T(8,128)(2,1)S(1)}, u32[]{:S(2)}, u32[]{:S(2)}) collective-permute-start(bf16[2,64,512]{2,1,0:T(8,128)(2,1)S(1)} %dynamic-slice_bitcast_fusion.9), channel_id=1, source_target_pairs={{0,4},{1,5},{2,6},{3,7},{4,0},{5,1},{6,2},{7,3},{8,12},{9,13},{10,... | collective-permute-start | bytes 393224 | tf_op jit(solution)/shard_map/ppermute | solution.py:293
  350.9 10.9 %collective-permute-start.39 = (bf16[64,512]{1,0:T(8,128)(2,1)S(1)}, bf16[64,512]{1,0:T(8,128)(2,1)S(1)}, u32[]{:S(2)}, u32[]{:S(2)}) collective-permute-start(bf16[64,512]{1,0:T(8,128)(2,1)S(1)} %dynamic-slice_bitcast_fusion.11), channel_id=1, source_target_pairs={{0,16},{1,17},{2,18},{3,19},{4,20},{5,21},{6,22},{7,23},{8,24},{9,... | collective-permute-start | bytes 196616 | tf_op jit(solution)/shard_map/ppermute | solution.py:293
  353.1 5.2 %collective-permute-start.29 = (bf16[64,512]{1,0:T(8,128)(2,1)S(1)}, bf16[64,512]{1,0:T(8,128)(2,1)S(1)}, u32[]{:S(2)}, u32[]{:S(2)}) collective-permute-start(bf16[64,512]{1,0:T(8,128)(2,1)S(1)} %dynamic-slice_bitcast_fusion.13), channel_id=1, source_target_pairs={{0,16},{1,17},{2,18},{3,19},{4,20},{5,21},{6,22},{7,23},{8,24},{9,... | collective-permute-start | bytes 196616 | tf_op jit(solution)/shard_map/ppermute | solution.py:293
  354.5 5.9 %collective-permute-start.34 = (bf16[64,512]{1,0:T(8,128)(2,1)S(1)}, bf16[64,512]{1,0:T(8,128)(2,1)S(1)}, u32[]{:S(2)}, u32[]{:S(2)}) collective-permute-start(bf16[64,512]{1,0:T(8,128)(2,1)S(1)} %dynamic-slice_bitcast_fusion.12), channel_id=1, source_target_pairs={{0,16},{1,17},{2,18},{3,19},{4,20},{5,21},{6,22},{7,23},{8,24},{9,... | collective-permute-start | bytes 196616 | tf_op jit(solution)/shard_map/ppermute | solution.py:293
